TPU v7x, 256 devices: a whole 4x4x8 slice. The times are simulated.
256 devices in a mesh: dp: 32 (over y, x, core), tensor: 8 (over z).
Axes of the slice: x: 4, y: 4, z: 8, core: 2. Of those that a mesh axis runs over, the one named last changes fastest.
Arguments:
- query_rows: bfloat16 [32768, 4096], P('dp', 'tensor'), may hold values from -128 to 128
- key_rows: bfloat16 [32768, 1024], P('dp', 'tensor'), may hold values from -5 to 5
- value_rows: bfloat16 [32768, 1024], P('dp', 'tensor'), may hold values from -6 to 6
- out_grad: bfloat16 [16384, 4096], P('dp', 'tensor'), may hold values from -12 to 12
- w_out: bfloat16 [4096, 4096], P('tensor'), may hold values from -0.09375 to 0.09375
- lengths: int32 [32, 32], replicated, may hold values from 0 to 32, as said below
- target: int32 [32, 32], replicated, may hold values from 0 to 31, as said below
Outputs:
- layer_out: bfloat16 [16384, 4096], P('dp', 'tensor')
- grad_queries: bfloat16 [32768, 4096], P('dp', 'tensor')
- grad_keys: bfloat16 [32768, 1024], P('dp', 'tensor')
- grad_values: bfloat16 [32768, 1024], P('dp', 'tensor')
- weight_grad: float32 [4096, 4096], P('tensor', 'dp')
Inputs may be any that keep to these rules, and one draw needn't show every extreme that they name: `lengths`: documents of a replica fill its pack from the first row in the order of j; some document has exactly 32 rows. `target`: each row is a permutation of the replicas. Every replica receives exactly 512 rows in all.
All inputs are finite; a program needn't handle non-finite values.
Results may differ from a plain program's by a relative error of at most 0.022.
Values may be sent and summed in bfloat16 or wider, within the bound.
A program may use at most 128 MiB of HBM per device.

v0:
```python
import jax
import jax.numpy as jnp
from jax import lax
from jax.sharding import PartitionSpec as P

HD = 128


neg_large = -1e30


def doc_tables(lengths, target):
    sources = lengths.shape[0]
    doc_ends = jnp.cumsum(lengths, axis=1)
    doc_starts = doc_ends - lengths
    replica_ids = jnp.arange(sources, dtype=jnp.int32)
    matches = (target[:, :, None] == replica_ids[None, None, :]).astype(jnp.int32)
    start_table = jnp.sum(matches * doc_starts[:, :, None], axis=1)
    length_table = jnp.sum(matches * lengths[:, :, None], axis=1)
    return (start_table, length_table)


def home_layout(start_row, length_row, piece_rows, home_rows):
    slot_ids = jnp.arange(piece_rows, dtype=jnp.int32)
    row_index = start_row[:, None] + slot_ids[None, :]
    is_live = slot_ids[None, :] < length_row[:, None]
    row_index = jnp.where(is_live, row_index, home_rows).reshape(-1)
    return (row_index, is_live.reshape(-1))


def balanced_layout(length_col, piece_rows, balanced_rows):
    sources = length_col.shape[0]
    col_ends = jnp.cumsum(length_col)
    col_starts = col_ends - length_col
    row_ids = jnp.arange(balanced_rows, dtype=jnp.int32)
    source_of = jnp.sum((row_ids[:, None] >= col_ends[None, :]).astype(jnp.int32), axis=1)
    matches = (source_of[:, None] == jnp.arange(sources, dtype=jnp.int32)[None, :]).astype(
        jnp.int32
    )
    begin_of = jnp.sum(matches * col_starts[None, :], axis=1)
    return source_of * piece_rows + row_ids - begin_of


def to_pieces(array, row_index, is_live, piece_rows):
    last_row = array.shape[0] - 1
    gathered = jnp.take(array, jnp.minimum(row_index, last_row), axis=0)
    gathered = jnp.where(is_live[:, None], gathered, jnp.zeros_like(gathered))
    return gathered.reshape(-1, piece_rows, array.shape[1])


def from_pieces(pieces, row_index, home_rows):
    flat_rows = pieces.reshape(-1, pieces.shape[2])
    output = jnp.zeros((home_rows, flat_rows.shape[1]), flat_rows.dtype)
    return output.at[row_index].set(flat_rows, mode="drop")


def allowed_mask(piece_len, piece_rows):
    slot_ids = jnp.arange(piece_rows, dtype=jnp.int32)
    causal = slot_ids[None, :] <= slot_ids[:, None]
    inside = slot_ids[None, None, :] < piece_len[:, None, None]
    diagonal = slot_ids[None, :] == slot_ids[:, None]
    return causal[None] & inside | diagonal[None]


def split_heads(query_pieces, key_pieces):
    sources, piece_rows, query_cols = query_pieces.shape
    kv_heads = key_pieces.shape[2] // HD
    group_size = query_cols // HD // kv_heads
    return (sources, piece_rows, query_cols, kv_heads, group_size)


def piece_forward(query_pieces, key_pieces, value_pieces, piece_len):
    sources, piece_rows, query_cols, kv_heads, group_size = split_heads(query_pieces, key_pieces)
    query_heads = query_pieces.reshape(sources, piece_rows, kv_heads, group_size, HD)
    key_heads = key_pieces.reshape(sources, piece_rows, kv_heads, HD)
    value_heads = value_pieces.reshape(sources, piece_rows, kv_heads, HD)
    scores = jnp.einsum(
        "bqcgh,bkch->bcgqk", query_heads, key_heads, preferred_element_type=jnp.float32
    ) * HD ** (-0.5)
    allowed = allowed_mask(piece_len, piece_rows)
    scores = jnp.where(allowed[:, None, None], scores, neg_large)
    row_max = jnp.max(scores, axis=-1, keepdims=True)
    weights = jnp.exp(scores - row_max)
    weights = weights / jnp.sum(weights, axis=-1, keepdims=True)
    context = jnp.einsum(
        "bcgqk,bkch->bqcgh",
        weights.astype(jnp.bfloat16),
        value_heads,
        preferred_element_type=jnp.float32,
    )
    return (context.astype(jnp.bfloat16).reshape(sources, piece_rows, query_cols), weights)


def piece_backward(query_pieces, key_pieces, value_pieces, context, dcontext, weights):
    sources, piece_rows, query_cols, kv_heads, group_size = split_heads(query_pieces, key_pieces)
    query_heads = query_pieces.reshape(sources, piece_rows, kv_heads, group_size, HD)
    key_heads = key_pieces.reshape(sources, piece_rows, kv_heads, HD)
    value_heads = value_pieces.reshape(sources, piece_rows, kv_heads, HD)
    context_heads = context.reshape(sources, piece_rows, kv_heads, group_size, HD)
    dcontext_heads = dcontext.reshape(sources, piece_rows, kv_heads, group_size, HD)
    dvalues = jnp.einsum(
        "bcgqk,bqcgh->bkch",
        weights.astype(jnp.bfloat16),
        dcontext_heads,
        preferred_element_type=jnp.float32,
    )
    dweights = jnp.einsum(
        "bqcgh,bkch->bcgqk", dcontext_heads, value_heads, preferred_element_type=jnp.float32
    )
    row_delta = jnp.sum(
        dcontext_heads.astype(jnp.float32) * context_heads.astype(jnp.float32), axis=-1
    )
    row_delta = jnp.transpose(row_delta, (0, 2, 3, 1))[..., None]
    dscores = (weights * (dweights - row_delta) * HD ** (-0.5)).astype(jnp.bfloat16)
    dqueries = jnp.einsum(
        "bcgqk,bkch->bqcgh", dscores, key_heads, preferred_element_type=jnp.float32
    )
    dkeys = jnp.einsum(
        "bcgqk,bqcgh->bkch", dscores, query_heads, preferred_element_type=jnp.float32
    )
    return (
        dqueries.astype(jnp.bfloat16).reshape(sources, piece_rows, query_cols),
        dkeys.astype(jnp.bfloat16).reshape(sources, piece_rows, kv_heads * HD),
        dvalues.astype(jnp.bfloat16).reshape(sources, piece_rows, kv_heads * HD),
    )


def fold_factory(context_rows, w_out, block_in):
    dcontext = lax.dot_general(
        block_in, w_out, (((1,), (1,)), ((), ())), preferred_element_type=jnp.float32
    )
    block_grad = lax.dot_general(
        context_rows, block_in, (((0,), (0,)), ((), ())), preferred_element_type=jnp.float32
    )
    return (dcontext, block_grad)


def shards(query_rows, key_rows, value_rows, out_grad, w_out, lengths, target):
    home_rows = query_rows.shape[0]
    balanced_rows = out_grad.shape[0]
    sources = lengths.shape[0]
    piece_rows = home_rows // sources
    query_cols = w_out.shape[0]
    own_index = lax.axis_index("dp")
    start_table, length_table = doc_tables(lengths, target)
    start_row = lax.dynamic_index_in_dim(start_table, own_index, 0, keepdims=False)
    length_row = lax.dynamic_index_in_dim(length_table, own_index, 0, keepdims=False)
    length_col = lax.dynamic_index_in_dim(length_table, own_index, 1, keepdims=False)
    row_index, is_live = home_layout(start_row, length_row, piece_rows, home_rows)
    balanced_index = balanced_layout(length_col, piece_rows, balanced_rows)
    query_pieces = to_pieces(query_rows, row_index, is_live, piece_rows)
    key_pieces = to_pieces(key_rows, row_index, is_live, piece_rows)
    value_pieces = to_pieces(value_rows, row_index, is_live, piece_rows)
    context, weights = piece_forward(query_pieces, key_pieces, value_pieces, length_row)
    flat_context = context.reshape(home_rows, query_cols)
    partial_value = jnp.dot(flat_context, w_out, preferred_element_type=jnp.float32)
    summed = lax.psum_scatter(
        partial_value.astype(jnp.bfloat16), "tensor", scatter_dimension=1, tiled=True
    )
    arrived = lax.all_to_all(
        summed.reshape(sources, piece_rows, -1), "dp", split_axis=0, concat_axis=0, tiled=True
    )
    layer_out = jnp.take(arrived.reshape(home_rows, -1), balanced_index, axis=0)
    spread = (
        jnp.zeros((home_rows, out_grad.shape[1]), jnp.bfloat16).at[balanced_index].set(out_grad)
    )
    fetched = lax.all_to_all(
        spread.reshape(sources, piece_rows, -1), "dp", split_axis=0, concat_axis=0, tiled=True
    )
    grad_rows = fetched.reshape(home_rows, -1)
    dcontext, weight_part = fold_factory(
        flat_context, w_out, lax.all_gather(grad_rows, "tensor", axis=1, tiled=True)
    )
    dcontext = dcontext.astype(jnp.bfloat16).reshape(sources, piece_rows, query_cols)
    dquery_pieces, dkey_pieces, dvalue_pieces = piece_backward(
        query_pieces, key_pieces, value_pieces, context, dcontext, weights
    )
    grad_queries = from_pieces(dquery_pieces, row_index, home_rows)
    grad_keys = from_pieces(dkey_pieces, row_index, home_rows)
    grad_values = from_pieces(dvalue_pieces, row_index, home_rows)
    weight_grad = lax.psum_scatter(
        weight_part.astype(jnp.bfloat16), "dp", scatter_dimension=1, tiled=True
    ).astype(jnp.float32)
    return (layer_out, grad_queries, grad_keys, grad_values, weight_grad)


def solution(mesh):
    return jax.shard_map(
        shards,
        mesh=mesh,
        in_specs=(
            P("dp", "tensor"),
            P("dp", "tensor"),
            P("dp", "tensor"),
            P("dp", "tensor"),
            P("tensor", None),
            P(),
            P(),
        ),
        out_specs=(
            P("dp", "tensor"),
            P("dp", "tensor"),
            P("dp", "tensor"),
            P("dp", "tensor"),
            P("tensor", "dp"),
        ),
        check_vma=False,
    )
```

profile of v0, /device:TPU:1, one launch (start us, length us, event | category | flops | bytes accessed | tf_op | source)
XLA Modules:
  0.0 350.5 jit_solution(9920784838466682318)
XLA Ops:
  10.8 3.2 scatter_custom_fusion
  14.1 25.7 %all_to_all.10 = bf16[32,32,512]{2,1,0:T(8,128)(2,1)} all-to-all(bf16[32,32,512]{2,1,0:T(8,128)(2,1)S(1)} %bitcast.115), channel_id=1, replica_groups=mesh['dp'=32,'tensor'=8] {'dp'}, dimensions={0} | all-to-all | bytes 2097152 | tf_op jit(solution)/shard_map/all_to_all | solution.py:167
  40.5 4.3 %gather_fusion.3 = bf16[1024,128]{1,0:T(8,128)(2,1)} fusion(bf16[1024,128]{1,0:T(8,128)(2,1)S(1)} %copy-done.1, s32[1024]{0:T(1024)S(1)} %fusion.37), kind=kCustom, calls=%fused_computation.1.clone | custom fusion | bytes 528384 | tf_op jit(solution)/shard_map/jit(_take)/gather | solution.py:46
  44.8 4.3 %gather_fusion.2 = bf16[1024,128]{1,0:T(8,128)(2,1)} fusion(bf16[1024,128]{1,0:T(8,128)(2,1)S(1)} %copy-done.2, s32[1024]{0:T(1024)S(1)} %fusion.37), kind=kCustom, calls=%fused_computation.clone | custom fusion | bytes 528384 | tf_op jit(solution)/shard_map/jit(_take)/gather | solution.py:46
  49.7 4.0 %gather_fusion = bf16[1024,512]{1,0:T(8,128)(2,1)S(1)} fusion(bf16[1024,512]{1,0:T(8,128)(2,1)S(1)} %copy-done, s32[1024]{0:T(1024)S(1)} %broadcast_clamp_fusion), kind=kCustom, calls=%fused_computation.2 | custom fusion | bytes 2101248 | tf_op jit(solution)/shard_map/jit(_take)/gather | solution.py:46
  54.2 2.2 select_select_fusion
  56.4 2.5 fusion.45
  60.2 1.7 fusion.25
  61.9 71.1 %all-gather.2.cloned.1.call-done = bf16[1024,4096]{1,0:T(8,128)(2,1)} async-done(((bf16[1024,512]{1,0:T(8,128)(2,1)}), bf16[1024,4096]{1,0:T(8,128)(2,1)}) %all-gather.2.cloned.1.call-update) | async-done | bytes 8388624 | tf_op jit(solution)/shard_map/all_gather | solution.py:172
  133.0 10.1 %convolution_convert_fusion.2 = bf16[1024,512]{1,0:T(8,128)(2,1)} fusion(bf16[1024,4096]{1,0:T(8,128)(2,1)} %all-gather.2.cloned.1.call-done, bf16[512,4096]{1,0:T(8,128)(2,1)} %param.13), kind=kOutput, calls=%fused_computation.20 | convolution fusion | flops 4295491584 | bytes 13631488 | tf_op jit(solution)/shard_map/dot_general | solution.py:129
  143.1 1.7 reshape.357
  144.8 3.0 fusion.3
  148.4 6.7 %convolution_convert_fusion = bf16[1024,4096]{1,0:T(8,128)(2,1)} fusion(bf16[512,4096]{1,0:T(8,128)(2,1)S(1)} %copy-done.15, bf16[128,8,4,128]{3,2,1,0:T(4,128)(2,1)S(1)} %bitcast.117), kind=kOutput, calls=%fused_computation.8 | convolution fusion | flops 4299161600 | bytes 13631488 | tf_op jit(solution)/shard_map/dot_general | solution.py:156
  155.4 9.5 %convolution_convert_fusion.1 = bf16[512,4096]{1,0:T(8,128)(2,1)} fusion(bf16[1024,4096]{1,0:T(8,128)(2,1)} %all-gather.2.cloned.1.call-done, bf16[128,8,4,128]{3,2,1,0:T(4,128)(2,1)S(1)} %bitcast.118), kind=kOutput, calls=%fused_computation.9 | convolution fusion | flops 4297064448 | bytes 13631488 | tf_op jit(solution)/shard_map/dot_general | solution.py:132
  164.9 6.6 %copy.47 = bf16[512,4096]{0,1:T(8,128)(2,1)} copy(bf16[512,4096]{1,0:T(8,128)(2,1)} %convolution_convert_fusion.1) | data formatting | bytes 8388608
  173.0 75.8 %reduce-scatter.5.cloned.1.call-done = bf16[1024,512]{1,0:T(8,128)(2,1)} async-done(((bf16[1024,4096]{1,0:T(8,128)(2,1)}), bf16[1024,512]{1,0:T(8,128)(2,1)}) %reduce-scatter.5.cloned.1.call-update) | async-done | bytes 1048592 | tf_op jit(solution)/shard_map/reduce_scatter | solution.py:157
  248.9 7.5 %all-to-all-start = ((bf16[32,32,512]{2,1,0:T(8,128)(2,1)}), bf16[32,32,512]{2,1,0:T(8,128)(2,1)S(1)}, u32[]{:S(2)}, u32[]{:S(2)}) async-start(bf16[32,32,512]{2,1,0:T(8,128)(2,1)} %bitcast.116), calls=%async_computation.1 | async-start | bytes 2097152 | tf_op jit(solution)/shard_map/all_to_all | solution.py:160
  256.3 3.6 %fusion.8 = bf16[32,4,32,32]{2,3,1,0:T(8,128)(2,1)S(1)} fusion(bf16[32,32,128,1]{2,1,3,0:T(8,128)(2,1)} %bitcast.122, f32[32,4,32]{2,1,0:T(4,128)} %bitcast.124, bf16[32,32,4,128]{3,2,1,0:T(4,128)(2,1)S(1)} %reshape.355, f32[32,4,32]{2,1,0:T(4,128)S(1)} %fusion.5, f32[32,1,4,32,32]{3,4,2,0,1:T(8,128)} %copy-done.3, f32[32,4,32]{2,1,0:T(4,128)S(1)} %get-tuple-element.18), kind=kOutput, calls=%fused_computation.25 | convolution fusion | flops 34340864 | bytes 2146304 | tf_op jit(solution)/shard_map/bqcgh,bkch->bcgqk/dot_general | solution.py:107
  263.3 4.0 %scatter_custom_fusion.3 = bf16[1024,128]{1,0:T(8,128)(2,1)} fusion(s32[1024]{0:T(1024)} %bitcast.130, bf16[1024,128]{1,0:T(8,128)(2,1)S(1)} %bitcast.134, bf16[]{:T(256)} %constant.55.clone.1), kind=kCustom, calls=%fused_computation.58 | custom fusion | bytes 262656 | tf_op jit(solution)/shard_map/scatter | solution.py:54
  267.3 6.3 %scatter_custom_fusion.1 = bf16[1024,512]{1,0:T(8,128)(2,1)} fusion(s32[1024]{0:T(1024)} %bitcast.131, bf16[128,8,4,128]{3,2,1,0:T(4,128)(2,1)S(1)} %bitcast.113, bf16[]{:T(256)} %constant.55.clone.1), kind=kCustom, calls=%fused_computation.30 | custom fusion | bytes 2097664 | tf_op jit(solution)/shard_map/scatter | solution.py:54
  273.6 2.2 fusion.9
  275.8 4.0 %scatter_custom_fusion.2 = bf16[1024,128]{1,0:T(8,128)(2,1)} fusion(s32[1024]{0:T(1024)} %bitcast.132, bf16[1024,128]{1,0:T(8,128)(2,1)S(1)} %bitcast.133, bf16[]{:T(256)} %constant.55.clone.1), kind=kCustom, calls=%fused_computation.60 | custom fusion | bytes 262656 | tf_op jit(solution)/shard_map/scatter | solution.py:54
  279.8 59.6 %reduce-scatter.7.cloned.1.call-done = bf16[128,512]{1,0:T(8,128)(2,1)} async-done(((bf16[4096,512]{1,0:T(8,128)(2,1)}), bf16[128,512]{1,0:T(8,128)(2,1)}) %reduce-scatter.7.cloned.1.call-update) | async-done | bytes 131088
  341.1 2.0 gather_fusion.1
  (74 shorter events, 15.1 us)
Async XLA Ops:
  7.2 42.5 %copy-start = (bf16[1024,512]{1,0:T(8,128)(2,1)S(1)}, bf16[1024,512]{1,0:T(8,128)(2,1)}, u32[]{:S(2)}) copy-start(bf16[1024,512]{1,0:T(8,128)(2,1)} %param.9) | copy-start | bytes 3145732
  7.2 125.8 %all-gather.2.cloned.1.call-start = ((), (), s32[]{:S(2)}) async-start(), calls=%async_computation.5 | async-start | bytes 9437184 | tf_op jit(solution)/shard_map/all_gather | solution.py:172
  10.8 28.9 %copy-start.10 = (s32[512,1]{0,1:T(1,128)}, s32[512,1]{0,1:T(1,128)S(1)}, u32[]{:S(2)}) copy-start(s32[512,1]{0,1:T(1,128)S(1)} %compare_select_fusion.3) | copy-start | bytes 6148
  10.8 29.6 %copy-start.1 = (bf16[1024,128]{1,0:T(8,128)(2,1)S(1)}, bf16[1024,128]{1,0:T(8,128)(2,1)}, u32[]{:S(2)}) copy-start(bf16[1024,128]{1,0:T(8,128)(2,1)} %param.10) | copy-start | bytes 786436
  39.7 5.0 %copy-start.2 = (bf16[1024,128]{1,0:T(8,128)(2,1)S(1)}, bf16[1024,128]{1,0:T(8,128)(2,1)}, u32[]{:S(2)}) copy-start(bf16[1024,128]{1,0:T(8,128)(2,1)} %param.11) | copy-start | bytes 786436
  39.8 209.1 %reduce-scatter.5.cloned.1.call-start = ((), (), s32[]{:S(2)}) async-start(), calls=%async_computation.4 | async-start | bytes 9437184 | tf_op jit(solution)/shard_map/reduce_scatter | solution.py:157
  40.1 16.3 %copy-start.12 = (pred[32,32]{1,0:T(8,128)(4,1)}, pred[32,32]{1,0:T(8,128)(4,1)S(1)}, u32[]{:S(2)}) copy-start(pred[32,32]{1,0:T(8,128)(4,1)S(1)} %get-tuple-element.14) | copy-start | bytes 3076
  54.0 4.9 %copy-start.6 = (bf16[32,32,4,128]{3,2,1,0:T(4,128)(2,1)}, bf16[32,32,4,128]{3,2,1,0:T(4,128)(2,1)S(1)}, u32[]{:S(2)}) copy-start(bf16[32,32,4,128]{3,2,1,0:T(4,128)(2,1)S(1)} %gather.14) | copy-start | bytes 3145732
  58.9 1.3 copy-start.3
  144.8 3.6 %copy-start.15 = (bf16[512,4096]{1,0:T(8,128)(2,1)S(1)}, bf16[512,4096]{1,0:T(8,128)(2,1)}, u32[]{:S(2)}) copy-start(bf16[512,4096]{1,0:T(8,128)(2,1)} %param.13) | copy-start | bytes 12582916
  155.1 184.2 %reduce-scatter.7.cloned.1.call-start = ((), (), s32[]{:S(2)}) async-start(), calls=%async_computation.6 | async-start | bytes 4325376
  171.5 0.7 copy-start.11
  171.5 1.2 copy-start.5
  173.0 86.9 %copy-start.7 = (bf16[32,32,4,128]{3,2,1,0:T(4,128)(2,1)}, bf16[32,32,4,128]{3,2,1,0:T(4,128)(2,1)S(1)}, u32[]{:S(2)}) copy-start(bf16[32,32,4,128]{3,2,1,0:T(4,128)(2,1)S(1)} %reshape.355) | copy-start | bytes 3145732
  248.9 92.2 %all-to-all-start = ((bf16[32,32,512]{2,1,0:T(8,128)(2,1)}), bf16[32,32,512]{2,1,0:T(8,128)(2,1)S(1)}, u32[]{:S(2)}, u32[]{:S(2)}) async-start(bf16[32,32,512]{2,1,0:T(8,128)(2,1)} %bitcast.116), calls=%async_computation.1 | async-start | bytes 2097152 | tf_op jit(solution)/shard_map/all_to_all | solution.py:160
  259.9 1.0 copy-start.9
  260.9 1.2 copy-start.4
  261.4 1.4 copy-start.8
  262.8 10.8 %copy-start.13 = (pred[32,32]{1,0:T(8,128)(4,1)S(1)}, pred[32,32]{1,0:T(8,128)(4,1)}, u32[]{:S(2)}) copy-start(pred[32,32]{1,0:T(8,128)(4,1)} %copy-done.12) | copy-start | bytes 3076
  341.1 2.0 copy-start.14
Sparse Core Ops, SparseCore 0:
  39.9 93.0 all-gather.1
  155.2 93.5 reduce-scatter.4
  252.8 86.4 reduce-scatter.6
where the time goes:
time: 352 us; the launch traced here: 351 us
  waiting for transfers between devices  207 us (59%)
  local copies, waits for them, and re-layouts  46.6 us (13%)
  matrix products  38.5 us (11%)
  blocking collectives  25.7 us (7%)
  between operations  14.1 us (4%)
  other arithmetic  11.1 us (3%)
  starting transfers between devices  8 us (2%)
    reduce_scatter x1, waiting for transfers between devices, shards(): lax.psum_scatter(partial_value.astype(jnp.bfloat16), 'tensor', scatter_di...  75.8 us
    all_gather x1, waiting for transfers between devices, shards(): lax.all_gather(grad_rows, 'tensor', axis=1, tiled=True)  71.1 us
    unnamed x4, waiting for transfers between devices  59.6 us
    all_to_all x1, blocking collectives, shards(): lax.all_to_all(spread.reshape(sources, piece_rows, -1), 'dp', split_axis=...  25.7 us
    scatter x3, local copies, waits for them, and re-layouts, from_pieces(): return output.at[row_index].set(flat_rows, mode='drop')  14.2 us
    gather x4, local copies, waits for them, and re-layouts, to_pieces(): gathered = jnp.take(array, jnp.minimum(row_index, last_row), axis=0)  12.9 us
    unnamed x34, local copies, waits for them, and re-layouts  10.8 us
    dot_general x1, matrix products, fold_factory(): lax.dot_general(block_in, w_out, (((1,), (1,)), ((), ())), preferred_elem...  10.1 us
  transfers between devices with their start and end apart: 4, of which 3 were waited for; matrix products, arithmetic and copies ran while one was open for 18% of the time, Pallas kernels for 0%

commit v1 on v0

--- a/solution.py
+++ b/solution.py
@@ -142,6 +142,7 @@
     piece_rows = home_rows // sources
     query_cols = w_out.shape[0]
     own_index = lax.axis_index("dp")
+    grad_rows = lax.all_gather(out_grad, "tensor", axis=1, tiled=True)
     start_table, length_table = doc_tables(lengths, target)
     start_row = lax.dynamic_index_in_dim(start_table, own_index, 0, keepdims=False)
     length_row = lax.dynamic_index_in_dim(length_table, own_index, 0, keepdims=False)
@@ -152,26 +153,25 @@
     key_pieces = to_pieces(key_rows, row_index, is_live, piece_rows)
     value_pieces = to_pieces(value_rows, row_index, is_live, piece_rows)
     context, weights = piece_forward(query_pieces, key_pieces, value_pieces, length_row)
-    flat_context = context.reshape(home_rows, query_cols)
-    partial_value = jnp.dot(flat_context, w_out, preferred_element_type=jnp.float32)
-    summed = lax.psum_scatter(
+    arrived = lax.all_to_all(context, "dp", split_axis=0, concat_axis=0, tiled=True)
+    balanced_context = jnp.take(arrived.reshape(home_rows, query_cols), balanced_index, axis=0)
+    partial_value = jnp.dot(balanced_context, w_out, preferred_element_type=jnp.float32)
+    layer_out = lax.psum_scatter(
         partial_value.astype(jnp.bfloat16), "tensor", scatter_dimension=1, tiled=True
     )
-    arrived = lax.all_to_all(
-        summed.reshape(sources, piece_rows, -1), "dp", split_axis=0, concat_axis=0, tiled=True
-    )
-    layer_out = jnp.take(arrived.reshape(home_rows, -1), balanced_index, axis=0)
+    dbalanced, weight_part = fold_factory(balanced_context, w_out, grad_rows)
     spread = (
-        jnp.zeros((home_rows, out_grad.shape[1]), jnp.bfloat16).at[balanced_index].set(out_grad)
-    )
-    fetched = lax.all_to_all(
-        spread.reshape(sources, piece_rows, -1), "dp", split_axis=0, concat_axis=0, tiled=True
-    )
-    grad_rows = fetched.reshape(home_rows, -1)
-    dcontext, weight_part = fold_factory(
-        flat_context, w_out, lax.all_gather(grad_rows, "tensor", axis=1, tiled=True)
-    )
-    dcontext = dcontext.astype(jnp.bfloat16).reshape(sources, piece_rows, query_cols)
+        jnp.zeros((home_rows, query_cols), jnp.bfloat16)
+        .at[balanced_index]
+        .set(dbalanced.astype(jnp.bfloat16))
+    )
+    dcontext = lax.all_to_all(
+        spread.reshape(sources, piece_rows, query_cols),
+        "dp",
+        split_axis=0,
+        concat_axis=0,
+        tiled=True,
+    )
     dquery_pieces, dkey_pieces, dvalue_pieces = piece_backward(
         query_pieces, key_pieces, value_pieces, context, dcontext, weights
     )

time: 352 us -> 295 us (0.84)
  waiting for transfers between devices: 207 us -> 180 us
  blocking collectives: 25.7 us -> 0 us
  matrix products: 38.5 us -> 31.8 us
  starting transfers between devices: 8 us -> 11.9 us
    all_gather x1, waiting for transfers between devices: 71.1 us -> 40.9 us  [shards(): grad_rows = lax.all_gather(out_grad, 'tensor', axis=1, tiled=True)]
    all_to_all x1 -> x2, waiting for transfers between devices: 0.01 us -> 28.5 us  [the longest x1 17 us: shards(): lax.all_to_all(context, 'dp', split_axis=0, concat_axis=0, tiled=True)]
    all_to_all x1 -> x0, blocking collectives: 25.7 us -> none  [shards(): lax.all_to_all(spread.reshape(sources, piece_rows, -1), 'dp', split_axis=...]
    reduce_scatter x1, waiting for transfers between devices: 75.8 us -> 58 us  [shards(): lax.psum_scatter(partial_value.astype(jnp.bfloat16), 'tensor', scatter_di...]
    unnamed x4, waiting for transfers between devices: 59.6 us -> 52.5 us
    dot_general x1, matrix products: 10.1 us -> 5.82 us  [fold_factory(): lax.dot_general(block_in, w_out, (((1,), (1,)), ((), ())), preferred_elem...]
    all_to_all x1 -> x2, starting transfers between devices: 7.48 us -> 11.6 us  [the longest x1 7.59 us: shards(): lax.all_to_all(spread.reshape(sources, piece_rows, query_cols), 'dp', spl...]
    unnamed x34 -> x24, local copies, waits for them, and re-layouts: 10.8 us -> 10.4 us
  transfers between devices with their start and end apart: 4 -> 5, of which waited for: 3 -> 5; matrix products, arithmetic and copies ran while one was open for 18% -> 19% of each run, Pallas kernels for 0% -> 0%
where the time goes in v1:
time: 295 us
  waiting for transfers between devices  180 us (61%)
  local copies, waits for them, and re-layouts  47.4 us (16%)
  matrix products  31.8 us (11%)
  between operations  14.1 us (5%)
  starting transfers between devices  11.9 us (4%)
  other arithmetic  9.54 us (3%)
    reduce_scatter x1, waiting for transfers between devices, shards(): lax.psum_scatter(partial_value.astype(jnp.bfloat16), 'tensor', scatter_di...  58 us
    unnamed x4, waiting for transfers between devices  52.5 us
    all_gather x1, waiting for transfers between devices, shards(): grad_rows = lax.all_gather(out_grad, 'tensor', axis=1, tiled=True)  40.9 us
    all_to_all x1, waiting for transfers between devices, shards(): lax.all_to_all(context, 'dp', split_axis=0, concat_axis=0, tiled=True)  17 us
    scatter x3, local copies, waits for them, and re-layouts, from_pieces(): return output.at[row_index].set(flat_rows, mode='drop')  14.2 us
    gather x4, local copies, waits for them, and re-layouts, to_pieces(): gathered = jnp.take(array, jnp.minimum(row_index, last_row), axis=0)  12.9 us
    all_to_all x1, waiting for transfers between devices, shards(): lax.all_to_all(spread.reshape(sources, piece_rows, query_cols), 'dp', spl...  11.5 us
    unnamed x24, local copies, waits for them, and re-layouts  10.4 us
  transfers between devices with their start and end apart: 5, of which 5 were waited for; matrix products, arithmetic and copies ran while one was open for 19% of the time, Pallas kernels for 0%

profile of v1, /device:TPU:1, one launch (start us, length us, event | category | flops | bytes accessed | tf_op | source)
XLA Modules:
  0.0 294.5 jit_solution(13190418357640654945)
XLA Ops:
  11.7 4.3 %gather_fusion.3 = bf16[1024,128]{1,0:T(8,128)(2,1)} fusion(bf16[1024,128]{1,0:T(8,128)(2,1)S(1)} %copy-done.1, s32[1024]{0:T(1024)S(1)} %fusion.35), kind=kCustom, calls=%fused_computation.1.clone | custom fusion | bytes 528384 | tf_op jit(solution)/shard_map/jit(_take)/gather | solution.py:46
  16.0 4.3 %gather_fusion.2 = bf16[1024,128]{1,0:T(8,128)(2,1)} fusion(bf16[1024,128]{1,0:T(8,128)(2,1)S(1)} %copy-done.2, s32[1024]{0:T(1024)S(1)} %fusion.35), kind=kCustom, calls=%fused_computation.clone | custom fusion | bytes 528384 | tf_op jit(solution)/shard_map/jit(_take)/gather | solution.py:46
  20.9 4.0 %gather_fusion = bf16[1024,512]{1,0:T(8,128)(2,1)S(1)} fusion(bf16[1024,512]{1,0:T(8,128)(2,1)S(1)} %copy-done, s32[1024]{0:T(1024)S(1)} %broadcast_clamp_fusion), kind=kCustom, calls=%fused_computation.2 | custom fusion | bytes 2101248 | tf_op jit(solution)/shard_map/jit(_take)/gather | solution.py:46
  25.4 2.2 select_select_fusion
  27.6 40.9 %all-gather.2.cloned.1.call-done = bf16[512,4096]{1,0:T(8,128)(2,1)} async-done(((bf16[512,512]{1,0:T(8,128)(2,1)}), bf16[512,4096]{1,0:T(8,128)(2,1)}) %all-gather.2.cloned.1.call-update) | async-done | bytes 4194320 | tf_op jit(solution)/shard_map/all_gather | solution.py:145
  68.5 5.8 %convolution_convert_fusion.4 = bf16[512,512]{1,0:T(8,128)(2,1)S(1)} fusion(bf16[512,4096]{1,0:T(8,128)(2,1)} %all-gather.2.cloned.1.call-done, bf16[512,4096]{1,0:T(8,128)(2,1)} %param.13), kind=kOutput, calls=%fused_computation.25 | convolution fusion | flops 2147745792 | bytes 8912896 | tf_op jit(solution)/shard_map/dot_general | solution.py:129
  74.3 3.5 %scatter_custom_fusion = bf16[1024,512]{1,0:T(8,128)(2,1)} fusion(s32[512]{0:T(512)S(1)} %bitcast.126, bf16[512,512]{1,0:T(8,128)(2,1)S(1)} %convolution_convert_fusion.4, bf16[]{:T(256)} %constant.55.clone.1), kind=kCustom, calls=%fused_computation.43 | custom fusion | bytes 1048578 | tf_op jit(solution)/shard_map/scatter | solution.py:166
  77.8 7.6 %all-to-all-start.1 = ((bf16[32,32,512]{2,1,0:T(8,128)(2,1)}), bf16[32,32,512]{2,1,0:T(8,128)(2,1)}, u32[]{:S(2)}, u32[]{:S(2)}) async-start(bf16[32,32,512]{2,1,0:T(8,128)(2,1)} %bitcast.23), calls=%async_computation.2 | async-start | bytes 2097152 | tf_op jit(solution)/shard_map/all_to_all | solution.py:168
  85.6 2.5 fusion.45
  91.1 11.5 %all-to-all-done.1 = bf16[32,32,512]{2,1,0:T(8,128)(2,1)} async-done(((bf16[32,32,512]{2,1,0:T(8,128)(2,1)}), bf16[32,32,512]{2,1,0:T(8,128)(2,1)}, u32[]{:S(2)}, u32[]{:S(2)}) %all-to-all-start.1) | async-done | bytes 1048608 | tf_op jit(solution)/shard_map/all_to_all | solution.py:168
  104.3 2.9 fusion.3
  109.0 4.0 %all-to-all-start = ((bf16[32,32,512]{2,1,0:T(8,128)(2,1)}), bf16[32,32,512]{2,1,0:T(8,128)(2,1)S(1)}, u32[]{:S(2)}, u32[]{:S(2)}) async-start(bf16[32,32,512]{2,1,0:T(8,128)(2,1)} %reshape.349), calls=%async_computation | async-start | bytes 2097152 | tf_op jit(solution)/shard_map/all_to_all | solution.py:156
  113.3 17.0 %all-to-all-done = bf16[32,32,512]{2,1,0:T(8,128)(2,1)S(1)} async-done(((bf16[32,32,512]{2,1,0:T(8,128)(2,1)}), bf16[32,32,512]{2,1,0:T(8,128)(2,1)S(1)}, u32[]{:S(2)}, u32[]{:S(2)}) %all-to-all-start) | async-done | bytes 1048608 | tf_op jit(solution)/shard_map/all_to_all | solution.py:156
  130.3 2.0 gather_fusion.1
  132.3 6.6 %convolution_convert_fusion = bf16[512,4096]{1,0:T(8,128)(2,1)} fusion(bf16[512,4096]{1,0:T(8,128)(2,1)} %all-gather.2.cloned.1.call-done, bf16[512,512]{1,0:T(8,128)(2,1)S(1)} %gather_fusion.1, pred[512]{0:T(512)(128)(4,1)S(1)} %compare_and_fusion.2), kind=kOutput, calls=%fused_computation.8 | convolution fusion | flops 2149842944 | bytes 8913408 | tf_op jit(solution)/shard_map/dot_general | solution.py:132
  138.9 6.5 %copy.45 = bf16[512,4096]{0,1:T(8,128)(2,1)} copy(bf16[512,4096]{1,0:T(8,128)(2,1)} %convolution_convert_fusion) | data formatting | bytes 8388608
  145.4 6.6 %convolution_convert_fusion.1 = bf16[512,4096]{1,0:T(8,128)(2,1)} fusion(bf16[512,4096]{1,0:T(8,128)(2,1)} %param.13, bf16[512,512]{1,0:T(8,128)(2,1)S(1)} %gather_fusion.1, pred[512]{0:T(512)(128)(4,1)S(1)} %compare_and_fusion.2), kind=kOutput, calls=%fused_computation.9 | convolution fusion | flops 2149842944 | bytes 8913408 | tf_op jit(solution)/shard_map/dot_general | solution.py:158
  153.6 3.1 %fusion.8 = bf16[32,4,32,32]{2,3,1,0:T(8,128)(2,1)S(1)} fusion(bf16[32,32,128,1]{2,1,3,0:T(8,128)(2,1)} %bitcast.121, f32[32,4,32]{2,1,0:T(4,128)} %bitcast.123, f32[32,4,32]{2,1,0:T(4,128)S(1)} %fusion.5, f32[32,1,4,32,32]{3,4,2,0,1:T(8,128)S(1)} %copy-done.4, f32[32,4,32]{2,1,0:T(4,128)S(1)} %get-tuple-element.18, bf16[32,32,512]{2,1,0:T(8,128)(2,1)} %all-to-all-done.1), kind=kOutput, calls=%fused_computation.24 | convolution fusion | flops 34340864 | bytes 2146304 | tf_op jit(solution)/shard_map/bqcgh,bkch->bcgqk/dot_general | solution.py:107
  158.4 1.9 fusion.10
  160.3 4.0 %scatter_custom_fusion.3 = bf16[1024,128]{1,0:T(8,128)(2,1)} fusion(s32[1024]{0:T(1024)} %bitcast.129, bf16[1024,128]{1,0:T(8,128)(2,1)S(1)} %bitcast.133, bf16[]{:T(256)} %constant.55.clone.1), kind=kCustom, calls=%fused_computation.56 | custom fusion | bytes 262656 | tf_op jit(solution)/shard_map/scatter | solution.py:54
  164.3 6.3 %scatter_custom_fusion.1 = bf16[1024,512]{1,0:T(8,128)(2,1)} fusion(s32[1024]{0:T(1024)} %bitcast.130, bf16[128,8,4,128]{3,2,1,0:T(4,128)(2,1)S(1)} %bitcast.117, bf16[]{:T(256)} %constant.55.clone.1), kind=kCustom, calls=%fused_computation.30 | custom fusion | bytes 2097664 | tf_op jit(solution)/shard_map/scatter | solution.py:54
  172.5 4.0 %scatter_custom_fusion.2 = bf16[1024,128]{1,0:T(8,128)(2,1)} fusion(s32[1024]{0:T(1024)} %bitcast.131, bf16[1024,128]{1,0:T(8,128)(2,1)S(1)} %bitcast.132, bf16[]{:T(256)} %constant.55.clone.1), kind=kCustom, calls=%fused_computation.58 | custom fusion | bytes 262656 | tf_op jit(solution)/shard_map/scatter | solution.py:54
  176.4 51.8 %reduce-scatter.7.cloned.1.call-done = bf16[128,512]{1,0:T(8,128)(2,1)} async-done(((bf16[4096,512]{1,0:T(8,128)(2,1)}), bf16[128,512]{1,0:T(8,128)(2,1)}) %reduce-scatter.7.cloned.1.call-update) | async-done | bytes 131088
  230.0 58.0 %reduce-scatter.5.cloned.1.call-done = bf16[512,512]{1,0:T(8,128)(2,1)} async-done(((bf16[512,4096]{1,0:T(8,128)(2,1)}), bf16[512,512]{1,0:T(8,128)(2,1)}) %reduce-scatter.5.cloned.1.call-update) | async-done | bytes 524304 | tf_op jit(solution)/shard_map/reduce_scatter | solution.py:159
  (64 shorter events, 19.4 us)
Async XLA Ops:
  7.2 13.8 %copy-start = (bf16[1024,512]{1,0:T(8,128)(2,1)S(1)}, bf16[1024,512]{1,0:T(8,128)(2,1)}, u32[]{:S(2)}) copy-start(bf16[1024,512]{1,0:T(8,128)(2,1)} %param.9) | copy-start | bytes 3145732
  7.2 4.5 %copy-start.1 = (bf16[1024,128]{1,0:T(8,128)(2,1)S(1)}, bf16[1024,128]{1,0:T(8,128)(2,1)}, u32[]{:S(2)}) copy-start(bf16[1024,128]{1,0:T(8,128)(2,1)} %param.10) | copy-start | bytes 786436
  7.2 8.8 %copy-start.2 = (bf16[1024,128]{1,0:T(8,128)(2,1)S(1)}, bf16[1024,128]{1,0:T(8,128)(2,1)}, u32[]{:S(2)}) copy-start(bf16[1024,128]{1,0:T(8,128)(2,1)} %param.11) | copy-start | bytes 786436
  7.2 61.3 %all-gather.2.cloned.1.call-start = ((), (), s32[]{:S(2)}) async-start(), calls=%async_computation.5 | async-start | bytes 4718592 | tf_op jit(solution)/shard_map/all_gather | solution.py:145
  11.0 74.6 %copy-start.9 = (pred[32,32]{1,0:T(8,128)(4,1)}, pred[32,32]{1,0:T(8,128)(4,1)S(1)}, u32[]{:S(2)}) copy-start(pred[32,32]{1,0:T(8,128)(4,1)S(1)} %get-tuple-element.14) | copy-start | bytes 3076
  25.2 60.4 %copy-start.6 = (bf16[32,32,4,128]{3,2,1,0:T(4,128)(2,1)}, bf16[32,32,4,128]{3,2,1,0:T(4,128)(2,1)S(1)}, u32[]{:S(2)}) copy-start(bf16[32,32,4,128]{3,2,1,0:T(4,128)(2,1)S(1)} %gather.14) | copy-start | bytes 3145732
  77.8 24.8 %all-to-all-start.1 = ((bf16[32,32,512]{2,1,0:T(8,128)(2,1)}), bf16[32,32,512]{2,1,0:T(8,128)(2,1)}, u32[]{:S(2)}, u32[]{:S(2)}) async-start(bf16[32,32,512]{2,1,0:T(8,128)(2,1)} %bitcast.23), calls=%async_computation.2 | async-start | bytes 2097152 | tf_op jit(solution)/shard_map/all_to_all | solution.py:168
  88.1 1.4 copy-start.3
  109.0 21.3 %all-to-all-start = ((bf16[32,32,512]{2,1,0:T(8,128)(2,1)}), bf16[32,32,512]{2,1,0:T(8,128)(2,1)S(1)}, u32[]{:S(2)}, u32[]{:S(2)}) async-start(bf16[32,32,512]{2,1,0:T(8,128)(2,1)} %reshape.349), calls=%async_computation | async-start | bytes 2097152 | tf_op jit(solution)/shard_map/all_to_all | solution.py:156
  113.0 115.3 %reduce-scatter.7.cloned.1.call-start = ((), (), s32[]{:S(2)}) async-start(), calls=%async_computation.6 | async-start | bytes 4325376
  145.4 142.6 %reduce-scatter.5.cloned.1.call-start = ((), (), s32[]{:S(2)}) async-start(), calls=%async_computation.4 | async-start | bytes 4718592 | tf_op jit(solution)/shard_map/reduce_scatter | solution.py:159
  152.0 1.6 copy-start.4
  156.7 1.1 copy-start.8
  156.8 1.6 copy-start.5
  158.4 12.2 %copy-start.7 = (bf16[32,32,4,128]{3,2,1,0:T(4,128)(2,1)S(1)}, bf16[32,32,4,128]{3,2,1,0:T(4,128)(2,1)}, u32[]{:S(2)}) copy-start(bf16[32,32,4,128]{3,2,1,0:T(4,128)(2,1)} %copy-done.6) | copy-start | bytes 3145732
  158.4 12.2 %copy-start.10 = (pred[32,32]{1,0:T(8,128)(4,1)S(1)}, pred[32,32]{1,0:T(8,128)(4,1)}, u32[]{:S(2)}) copy-start(pred[32,32]{1,0:T(8,128)(4,1)} %copy-done.9) | copy-start | bytes 3076
Sparse Core Ops, SparseCore 0:
  9.8 58.6 all-gather.1
  145.5 82.7 reduce-scatter.6
  231.6 56.3 reduce-scatter.4

commit v2 on v1

v2 whole, which is shorter than its diff:
```python
import jax
import jax.numpy as jnp
from jax import lax
from jax.experimental import pallas as pl
from jax.experimental.pallas import tpu as pltpu
from jax.sharding import PartitionSpec as P

HD = 128
GROUP = 4
QC = GROUP * HD
XC = QC + 2 * HD
SLOT = 32
NDP = 32
NCHIP = NDP // 2
NT = 8
PACK = NDP * SLOT
CAP = 512
MC = 512
TILE = 128
HALF = CAP // 2
SCALE = HD**-0.5
OFF = 4096.0
BF = jnp.bfloat16
F32 = jnp.float32
MESH = pl.DeviceIdType.MESH


def nn(a, b):
    return lax.dot_general(a, b, (((1,), (0,)), ((), ())), preferred_element_type=F32)


def nt(a, b):
    return lax.dot_general(a, b, (((1,), (1,)), ((), ())), preferred_element_type=F32)


def tn(a, b):
    return lax.dot_general(a, b, (((0,), (0,)), ((), ())), preferred_element_type=F32)


def iota(shape, dim):
    return lax.broadcasted_iota(jnp.int32, shape, dim)


def one_hot(mask):
    return jnp.where(mask, 1.0, 0.0).astype(BF)


def remote(src, dst, send, recv, where):
    return pltpu.make_async_remote_copy(
        src_ref=src, dst_ref=dst, send_sem=send, recv_sem=recv, device_id=where, device_id_type=MESH
    )


def slot_index(member, starts, sizes):
    high = jnp.floor(starts * (1.0 / SLOT))
    low = starts - high * SLOT
    slot_col = (iota((PACK, 1), 0) % SLOT).astype(F32)
    slot_row = (iota((1, PACK), 1) % SLOT).astype(F32)
    start_col = jnp.sum(jnp.where(member, starts[0:1], 0.0), axis=1, keepdims=True)
    size_col = jnp.sum(jnp.where(member, sizes[0:1], 0.0), axis=1, keepdims=True)
    picks = one_hot(member)
    start_row = nt(high.astype(BF), picks)[0:1] * SLOT + nt(low.astype(BF), picks)[0:1]
    size_row = nt(sizes.astype(BF), picks)[0:1]
    col = jnp.where(slot_col < size_col, start_col + slot_col, OFF)
    row = jnp.where(slot_row < size_row, start_row + slot_row, OFF)
    return col, row


def kernel(
    q_in, k_in, v_in, og_in, w_in, len_ref, tgt_ref,
    lo_ref, gq_ref, gk_ref, gv_ref, wg_ref,
    home, pieces, og, w, perm, perm_t, sel, sel_t, home_col, home_row, bal_col, bal_row, bias, probs,
    ctx_send, ctx_recv, bctx, bctx_t, part, rs_recv, dbal, wp, sx, wr, d_send, d_recv, gp,
    load_sem, ag_send, ag_recv, rs_send, rs_recv_sem, c_send, c_recv, d_ssem, d_rsem,
    x_send, x_recv, w_send, w_recv,
):
    me = lax.axis_index("dp")
    z = lax.axis_index("tensor")
    core = lax.rem(me, 2)
    chip = lax.div(me, 2)
    right, left = {"tensor": lax.rem(z + 1, NT)}, {"tensor": lax.rem(z + NT - 1, NT)}
    toward = (right, left)
    sibling = {"dp": me + 1 - 2 * core}

    loads = [
        pltpu.make_async_copy(q_in, home.at[:, pl.ds(0, QC)], load_sem.at[0]),
        pltpu.make_async_copy(k_in, home.at[:, pl.ds(QC, HD)], load_sem.at[1]),
        pltpu.make_async_copy(v_in, home.at[:, pl.ds(QC + HD, HD)], load_sem.at[2]),
        pltpu.make_async_copy(og_in, og.at[0], load_sem.at[3]),
        pltpu.make_async_copy(w_in, w, load_sem.at[4]),
    ]
    for one in (loads[3], loads[0], loads[1], loads[2], loads[4]):
        one.start()

    barrier = pltpu.get_barrier_semaphore()
    pl.semaphore_signal(barrier, inc=1, device_id=right, device_id_type=MESH)
    pl.semaphore_signal(barrier, inc=1, device_id=left, device_id_type=MESH)

    @pl.loop(1, NDP)
    def _(k):
        pl.semaphore_signal(
            barrier, inc=1, device_id={"dp": lax.rem(me + k, NDP)}, device_id_type=MESH
        )

    pl.semaphore_wait(barrier, NDP + 1)

    halves = (pl.ds(0, HALF), pl.ds(HALF, HALF))

    def ag_copy(way, step, half):
        src = (NT - step) % NT if way == 0 else step
        dst = (NT - step - 1) % NT if way == 0 else step + 1
        return remote(
            og.at[src, halves[half]],
            og.at[dst, halves[half]],
            ag_send.at[way, step, half],
            ag_recv.at[way, step, half],
            toward[way],
        )

    def ag_halves(way, step):
        return (0, 1) if step < 3 else (way,)

    def ag_step(step):
        for half in (0, 1):
            for way in (0, 1):
                if step > 0:
                    ag_copy(way, step - 1, half if way == 0 else 1 - half).wait_recv()
                order = half if way == 0 else 1 - half
                if order in ag_halves(way, step):
                    ag_copy(way, step, order).start()

    loads[3].wait()
    ag_step(0)

    lane = iota((NDP, NDP), 1)
    before = jnp.where(iota((NDP, NDP), 0) < lane, 1.0, 0.0).astype(BF)
    sizes = jnp.broadcast_to(len_ref[pl.ds(me, 1), :].astype(F32), (8, NDP))
    starts = nn(sizes.astype(BF), before)
    doc_of = lax.div(iota((PACK, NDP), 0), SLOT)
    col, row = slot_index(tgt_ref[pl.ds(me, 1), :] == doc_of, starts, sizes)
    home_col[...] = jnp.broadcast_to(col, (PACK, 128))
    home_row[...] = jnp.broadcast_to(row, (8, PACK))

    @pl.loop(0, PACK // TILE)
    def _(i):
        rows = pl.ds(pl.multiple_of(i * TILE, TILE), TILE)
        index = home_col[rows, 0:1]
        perm[rows, :] = one_hot(index == iota((TILE, PACK), 1).astype(F32))

    for one in loads[:3]:
        one.wait()

    @pl.loop(0, XC // 256)
    def _(i):
        cols = pl.ds(pl.multiple_of(i * 256, 256), 256)
        pieces[:, cols] = nn(perm[...], home[:, cols]).astype(BF)

    key_row = iota((TILE, QC), 0)
    query_row = iota((TILE, QC), 1) % TILE
    allowed = (lax.div(key_row, SLOT) == lax.div(query_row, SLOT)) & (key_row <= query_row)
    bias[...] = jnp.where(allowed, 0.0, -1e30)

    def heads(ref, rows):
        return jnp.concatenate([ref[rows, h * HD : (h + 1) * HD] for h in range(GROUP)], axis=0)

    @pl.loop(0, PACK // TILE)
    def _(i):
        rows = pl.ds(pl.multiple_of(i * TILE, TILE), TILE)
        scores = nt(pieces[rows, QC : QC + HD], heads(pieces, rows)) * SCALE + bias[...]
        weights = jnp.exp(scores - jnp.max(scores, axis=0, keepdims=True))
        weights = weights / jnp.sum(weights, axis=0, keepdims=True)
        probs[i] = weights
        context = tn(weights.astype(BF), pieces[rows, QC + HD : XC]).astype(BF)
        for h in range(GROUP):
            ctx_send[rows, h * HD : (h + 1) * HD] = context[h * TILE : (h + 1) * TILE]

    def piece(d):
        return pl.ds(pl.multiple_of(d * SLOT, SLOT), SLOT)

    def exchange_start(source, dest, send, recv):
        @pl.loop(1, NDP)
        def _(k):
            d = lax.rem(me + k, NDP)
            remote(
                source.at[piece(d)], dest.at[piece(me)], send.at[d], recv.at[me], {"dp": d}
            ).start()

        dest[piece(me), :] = source[piece(me), :]

    def exchange_wait(source, dest, send, recv):
        @pl.loop(1, NDP)
        def _(k):
            d = lax.rem(me + k, NDP)
            remote(
                source.at[piece(d)], dest.at[piece(d)], send.at[d], recv.at[d], {"dp": d}
            ).wait()

    exchange_start(ctx_send, ctx_recv, c_send, c_recv)

    sent_here = jnp.where(tgt_ref[...] == me, len_ref[...], 0).astype(F32).astype(BF)
    sizes = nt(jnp.ones((8, NDP), BF), sent_here)
    starts = nn(sizes.astype(BF), before)
    col, row = slot_index(iota((PACK, NDP), 1) == doc_of, starts, sizes)
    bal_col[...] = jnp.broadcast_to(col, (PACK, 128))
    bal_row[...] = jnp.broadcast_to(row, (8, PACK))

    @pl.loop(0, CAP // TILE)
    def _(i):
        rows = pl.ds(pl.multiple_of(i * TILE, TILE), TILE)
        here = (iota((TILE, PACK), 0) + i * TILE).astype(F32)
        sel[rows, :] = one_hot(bal_row[0:1, :] == here)

    loads[4].wait()
    ag_step(1)

    def model_cols(rel):
        owner = lax.rem(z + rel, NT)
        return owner, pl.ds(pl.multiple_of(owner * MC, MC), MC)

    def add_dbalanced(rel, first=False):
        _, cols = model_cols(rel)
        term = nt(og[rel], w[:, cols])
        dbal[...] = term if first else dbal[...] + term

    add_dbalanced(0, True)
    add_dbalanced(1)
    add_dbalanced(7)

    @pl.loop(0, PACK // TILE)
    def _(i):
        rows = pl.ds(pl.multiple_of(i * TILE, TILE), TILE)
        here = (iota((TILE, PACK), 0) + i * TILE).astype(F32)
        perm_t[rows, :] = one_hot(home_row[0:1, :] == here)
        index = bal_col[rows, 0:1]
        sel_t[rows, :] = one_hot(index == iota((TILE, CAP), 1).astype(F32))

    ag_step(2)
    add_dbalanced(2)
    add_dbalanced(6)

    exchange_wait(ctx_send, ctx_recv, c_send, c_recv)
    balanced = nn(sel[...], ctx_recv[...]).astype(BF)
    bctx[...] = balanced
    bctx_t[...] = balanced.T

    def project(rel):
        _, cols = model_cols(rel)
        part[rel] = nn(bctx[...], w[:, cols]).astype(BF)

    def rs_copy(way, step, half):
        rel = 4 - step if way == 0 else 4 + step
        return remote(
            part.at[rel, halves[half]],
            rs_recv.at[way, step, halves[half]],
            rs_send.at[way, step, half],
            rs_recv_sem.at[way, step, half],
            toward[way],
        )

    def rs_step(step, late=False):
        for half in (0, 1):
            for way in (0, 1):
                order = half if way == 0 else 1 - half
                rel = 4 - step if way == 0 else 4 + step
                if order in ag_halves(way, 3 if step == 1 else 0):
                    rs_copy(way, step - 1, order).wait_recv()
                    rows = halves[order]
                    total = part[rel, rows].astype(F32) + rs_recv[way, step - 1, rows].astype(F32)
                    part[rel, rows] = total.astype(BF)
                    rs_copy(way, step, order).start()

    def weight_block(rel):
        owner, _ = model_cols(rel)
        grad = nn(bctx_t[...], og[rel]).astype(BF)
        for j in range(4):
            wp[lax.rem(core + j, 2), 2 * owner + j // 2] = grad[:, j * 128 : (j + 1) * 128]

    def sibling_copy(rel):
        owner, _ = model_cols(rel)
        both = pl.ds(2 * owner, 2)
        return remote(wp.at[1, both], sx.at[both], x_send.at[rel], x_recv.at[rel], sibling)

    def weight_copy(m, slot):
        return remote(
            wp.at[0, m], wr.at[slot], w_send.at[m], w_recv.at[slot], {"dp": 2 * m + core}
        )

    def weight_send(rel):
        owner, _ = model_cols(rel)
        sibling_copy(rel).wait_recv()
        for j in range(2):
            m = 2 * owner + j
            total = (wp[0, m].astype(F32) + sx[m].astype(F32)).astype(BF)
            wp[0, m] = total

            @pl.when(m != chip)
            def _():
                weight_copy(m, chip).start()

            @pl.when(m == chip)
            def _():
                wr[m] = total

    project(4)
    rs_copy(0, 0, 0).start()
    rs_copy(1, 0, 1).start()
    for rel in (0, 1, 7):
        weight_block(rel)
        sibling_copy(rel).start()
    ag_step(3)
    project(3)
    project(5)
    add_dbalanced(3)
    add_dbalanced(5)
    for rel in (2, 6):
        weight_block(rel)
        sibling_copy(rel).start()
    for rel in (0, 1, 7):
        weight_send(rel)
    ag_copy(0, 3, 0).wait_recv()
    ag_copy(1, 3, 1).wait_recv()
    rs_copy(0, 1, 1).start()
    rs_copy(1, 1, 0).start()
    add_dbalanced(4)
    d_send[...] = nn(sel_t[...], dbal[...].astype(BF)).astype(BF)
    exchange_start(d_send, d_recv, d_ssem, d_rsem)
    rs_step(1)
    for rel in (3, 5, 4):
        weight_block(rel)
        sibling_copy(rel).start()
    project(2)
    project(6)
    for rel in (2, 6):
        weight_send(rel)
    rs_step(2)
    project(1)
    project(7)
    for rel in (3, 5, 4):
        weight_send(rel)
    project(0)
    exchange_wait(d_send, d_recv, d_ssem, d_rsem)

    def backward(low, high):
        @pl.loop(low, high)
        def _(i):
            rows = pl.ds(pl.multiple_of(i * TILE, TILE), TILE)
            weights = probs[i]
            half = weights.astype(BF)
            dcontext = heads(d_recv, rows)
            dweights = nt(pieces[rows, QC + HD : XC], dcontext)
            delta = jnp.sum(half.astype(F32) * dweights, axis=0, keepdims=True)
            dscores = (weights * (dweights - delta) * SCALE).astype(BF)
            dq = tn(dscores, pieces[rows, QC : QC + HD]).astype(BF)
            for h in range(GROUP):
                gp[rows, h * HD : (h + 1) * HD] = dq[h * TILE : (h + 1) * TILE]
            gp[rows, QC : QC + HD] = nn(dscores, heads(pieces, rows)).astype(BF)
            gp[rows, QC + HD : XC] = nn(half, dcontext).astype(BF)

    backward(0, 4)
    rs_step(3)
    backward(4, 8)

    @pl.loop(0, QC // 256)
    def _(i):
        cols = pl.ds(pl.multiple_of(i * 256, 256), 256)
        gq_ref[:, cols] = nn(perm_t[...], gp[:, cols]).astype(BF)

    both = nn(perm_t[...], gp[:, QC:XC]).astype(BF)
    gk_ref[...] = both[:, :HD]
    gv_ref[...] = both[:, HD:]

    @pl.loop(1, NCHIP)
    def _(k):
        m = lax.rem(chip + k, NCHIP)
        weight_copy(m, m).wait()

    total = wr[0].astype(F32)
    for m in range(1, NCHIP):
        total = total + wr[m].astype(F32)
    wg_ref[...] = total

    for way in (0, 1):
        for half in (0, 1):
            rs_copy(way, 3, half).wait_recv()
    total = part[0].astype(F32) + rs_recv[0, 3].astype(F32) + rs_recv[1, 3].astype(F32)
    lo_ref[...] = total.astype(BF)

    for way in (0, 1):
        for step in range(4):
            for half in (0, 1):
                if half in ag_halves(way, step):
                    ag_copy(way, step, half).wait_send()
                if half in ag_halves(way, 3 - step):
                    rs_copy(way, step, half).wait_send()
    for rel in range(NT):
        sibling_copy(rel).wait_send()


def shards(query_rows, key_rows, value_rows, out_grad, w_out, lengths, target):
    vmem = pl.BlockSpec(memory_space=pltpu.VMEM)
    hbm = pl.BlockSpec(memory_space=pl.ANY)
    dma = pltpu.SemaphoreType.DMA
    outs = (
        jax.ShapeDtypeStruct((CAP, MC), BF),
        jax.ShapeDtypeStruct((PACK, QC), BF),
        jax.ShapeDtypeStruct((PACK, HD), BF),
        jax.ShapeDtypeStruct((PACK, HD), BF),
        jax.ShapeDtypeStruct((QC, 128), F32),
    )
    scratch = [
        pltpu.VMEM((PACK, XC), BF),
        pltpu.VMEM((PACK, XC), BF),
        pltpu.VMEM((NT, CAP, MC), BF),
        pltpu.VMEM((QC, NT * MC), BF),
        pltpu.VMEM((PACK, PACK), BF),
        pltpu.VMEM((PACK, PACK), BF),
        pltpu.VMEM((CAP, PACK), BF),
        pltpu.VMEM((PACK, CAP), BF),
        pltpu.VMEM((PACK, 128), F32),
        pltpu.VMEM((8, PACK), F32),
        pltpu.VMEM((PACK, 128), F32),
        pltpu.VMEM((8, PACK), F32),
        pltpu.VMEM((TILE, QC), F32),
        pltpu.VMEM((PACK // TILE, TILE, QC), F32),
        pltpu.VMEM((PACK, QC), BF),
        pltpu.VMEM((PACK, QC), BF),
        pltpu.VMEM((CAP, QC), BF),
        pltpu.VMEM((QC, CAP), BF),
        pltpu.VMEM((NT, CAP, MC), BF),
        pltpu.VMEM((2, 4, CAP, MC), BF),
        pltpu.VMEM((CAP, QC), F32),
        pltpu.VMEM((2, NCHIP, QC, 128), BF),
        pltpu.VMEM((NCHIP, QC, 128), BF),
        pltpu.VMEM((NCHIP, QC, 128), BF),
        pltpu.VMEM((PACK, QC), BF),
        pltpu.VMEM((PACK, QC), BF),
        pltpu.VMEM((PACK, XC), BF),
        dma((5,)),
        dma((2, 4, 2)),
        dma((2, 4, 2)),
        dma((2, 4, 2)),
        dma((2, 4, 2)),
        dma((NDP,)),
        dma((NDP,)),
        dma((NDP,)),
        dma((NDP,)),
        dma((NT,)),
        dma((NT,)),
        dma((NCHIP,)),
        dma((NCHIP,)),
    ]
    return pl.pallas_call(
        kernel,
        out_shape=outs,
        in_specs=[hbm, hbm, hbm, hbm, hbm, vmem, vmem],
        out_specs=(vmem,) * 5,
        scratch_shapes=scratch,
        compiler_params=pltpu.CompilerParams(
            collective_id=0, has_side_effects=True, vmem_limit_bytes=60 * 2**20
        ),
    )(query_rows, key_rows, value_rows, out_grad, w_out, lengths, target)


def solution(mesh):
    return jax.shard_map(
        shards,
        mesh=mesh,
        in_specs=(
            P("dp", "tensor"),
            P("dp", "tensor"),
            P("dp", "tensor"),
            P("dp", "tensor"),
            P("tensor", None),
            P(),
            P(),
        ),
        out_specs=(
            P("dp", "tensor"),
            P("dp", "tensor"),
            P("dp", "tensor"),
            P("dp", "tensor"),
            P("tensor", "dp"),
        ),
        check_vma=False,
    )
```

time: 295 us -> 120 us (0.41)
  waiting for transfers between devices: 180 us -> 0 us
  Pallas kernels: 0 us -> 111 us
  local copies, waits for them, and re-layouts: 47.4 us -> 8.22 us
  matrix products: 31.8 us -> 0 us
  between operations: 14.1 us -> 0.65 us
  starting transfers between devices: 11.9 us -> 0 us
  other arithmetic: 9.54 us -> 0 us
    pallas_call x0 -> x1, Pallas kernels: none -> 111 us  [shards(): pl.pallas_call(kernel, out_shape=outs, in_specs=[hbm, hbm, hbm, hbm, hbm,...]
    reduce_scatter x1 -> x0, waiting for transfers between devices: 58 us -> none  [shards(): lax.psum_scatter(partial_value.astype(jnp.bfloat16), 'tensor', scatter_di...]
    unnamed x4 -> x0, waiting for transfers between devices: 52.5 us -> none
    all_gather x1 -> x0, waiting for transfers between devices: 40.9 us -> none  [shards(): grad_rows = lax.all_gather(out_grad, 'tensor', axis=1, tiled=True)]
    dot_general x9 -> x0, matrix products: 31.8 us -> none  [the longest x1 6.63 us: fold_factory(): lax.dot_general(context_rows, block_in, (((0,), (0,)), ((), ())), preferr...]
    all_to_all x2 -> x0, waiting for transfers between devices: 28.5 us -> none  [the longest x1 17 us: shards(): lax.all_to_all(context, 'dp', split_axis=0, concat_axis=0, tiled=True)]
    scatter x4 -> x0, local copies, waits for them, and re-layouts: 17.7 us -> none  [the longest x3 14.2 us: from_pieces(): return output.at[row_index].set(flat_rows, mode='drop')]
    gather x5 -> x0, local copies, waits for them, and re-layouts: 14.8 us -> none  [the longest x4 12.9 us: to_pieces(): gathered = jnp.take(array, jnp.minimum(row_index, last_row), axis=0)]
  transfers between devices with their start and end apart: 5 -> 0, of which waited for: 5 -> 0; matrix products, arithmetic and copies ran while one was open for 19% -> 0% of each run, Pallas kernels for 0% -> 0%
where the time goes in v2:
time: 120 us
  Pallas kernels  111 us (92%)
  local copies, waits for them, and re-layouts  8.22 us (7%)
    pallas_call x1, Pallas kernels, shards(): pl.pallas_call(kernel, out_shape=outs, in_specs=[hbm, hbm, hbm, hbm, hbm,...  111 us
    unnamed x7, local copies, waits for them, and re-layouts  8.22 us

profile of v2, /device:TPU:1, one launch (start us, length us, event | category | flops | bytes accessed | tf_op | source)
XLA Modules:
  0.0 119.6 jit_solution(10642774095071538579)
XLA Ops:
  0.6 110.7 %shard_map.110 = (bf16[512,512]{1,0:T(8,128)(2,1)}, bf16[1024,512]{1,0:T(8,128)(2,1)}, bf16[1024,128]{1,0:T(8,128)(2,1)}, bf16[1024,128]{1,0:T(8,128)(2,1)}, f32[512,128]{1,0:T(8,128)}) custom-call(bf16[1024,512]{1,0:T(8,128)(2,1)} %q_in.1, bf16[1024,128]{1,0:T(8,128)(2,1)} %k_in.1, bf16[1024,128]{1,0:T(8,128)(2,1)} %v_in.1, bf16[512,512]{1,0:T(8,128)(2,1)} %og_in.1, ...), custom_call_target="tpu_custom_call" | custom-call | tf_op jit(solution)/shard_map/pallas_call | solution.py:452
  111.4 0.0 copy-start
  111.4 1.9 %copy.17 = bf16[512,512]{1,0:T(8,128)(2,1)} copy(bf16[512,512]{1,0:T(8,128)(2,1)} %get-tuple-element.10) | data formatting | bytes 1048576
  113.3 2.3 %copy.18 = bf16[1024,512]{1,0:T(8,128)(2,1)} copy(bf16[1024,512]{1,0:T(8,128)(2,1)} %get-tuple-element.11) | data formatting | bytes 2097152
  115.6 1.7 %copy.19 = bf16[1024,128]{1,0:T(8,128)(2,1)} copy(bf16[1024,128]{1,0:T(8,128)(2,1)} %get-tuple-element.12) | data formatting | bytes 524288
  117.2 1.7 %copy.20 = bf16[1024,128]{1,0:T(8,128)(2,1)} copy(bf16[1024,128]{1,0:T(8,128)(2,1)} %get-tuple-element.13) | data formatting | bytes 524288
  118.9 0.0 copy-done
  118.9 0.7 copy.21
Async XLA Ops:
  111.4 7.5 %copy-start = (f32[512,128]{1,0:T(8,128)S(1)}, f32[512,128]{1,0:T(8,128)}, u32[]{:S(2)}) copy-start(f32[512,128]{1,0:T(8,128)} %get-tuple-element.14) | copy-start | bytes 786436

commit v3 on v2

--- a/solution.py
+++ b/solution.py
@@ -68,11 +68,13 @@
 
 def kernel(
     q_in, k_in, v_in, og_in, w_in, len_ref, tgt_ref,
-    lo_ref, gq_ref, gk_ref, gv_ref, wg_ref,
+    lo_out, gq_out, gk_out, gv_out, wg_out,
     home, pieces, og, w, perm, perm_t, sel, sel_t, home_col, home_row, bal_col, bal_row, bias, probs,
-    ctx_send, ctx_recv, bctx, bctx_t, part, rs_recv, dbal, wp, sx, wr, d_send, d_recv, gp,
+    ctx_send, ctx_recv, bctx, bctx_t, part, rs_recv, dbal, wp, sx, wsum, wfar, wnear, vsum, vfar, vnear,
+    d_send, d_recv, gp,
+    lo, gq, gk, gv, wg,
     load_sem, ag_send, ag_recv, rs_send, rs_recv_sem, c_send, c_recv, d_ssem, d_rsem,
-    x_send, x_recv, w_send, w_recv,
+    x_send, x_recv, w_send, w_recv, store_sem,
 ):
     me = lax.axis_index("dp")
     z = lax.axis_index("tensor")
@@ -120,8 +122,8 @@
     def ag_halves(way, step):
         return (0, 1) if step < 3 else (way,)
 
-    def ag_step(step):
-        for half in (0, 1):
+    def ag_step(step, parts=(0, 1)):
+        for half in parts:
             for way in (0, 1):
                 if step > 0:
                     ag_copy(way, step - 1, half if way == 0 else 1 - half).wait_recv()
@@ -163,8 +165,7 @@
     def heads(ref, rows):
         return jnp.concatenate([ref[rows, h * HD : (h + 1) * HD] for h in range(GROUP)], axis=0)
 
-    @pl.loop(0, PACK // TILE)
-    def _(i):
+    def forward(i):
         rows = pl.ds(pl.multiple_of(i * TILE, TILE), TILE)
         scores = nt(pieces[rows, QC : QC + HD], heads(pieces, rows)) * SCALE + bias[...]
         weights = jnp.exp(scores - jnp.max(scores, axis=0, keepdims=True))
@@ -174,6 +175,10 @@
         for h in range(GROUP):
             ctx_send[rows, h * HD : (h + 1) * HD] = context[h * TILE : (h + 1) * TILE]
 
+    pl.loop(0, 4)(forward)
+    ag_step(1, (0,))
+    pl.loop(4, 8)(forward)
+
     def piece(d):
         return pl.ds(pl.multiple_of(d * SLOT, SLOT), SLOT)
 
@@ -196,6 +201,7 @@
             ).wait()
 
     exchange_start(ctx_send, ctx_recv, c_send, c_recv)
+    ag_step(1, (1,))
 
     sent_here = jnp.where(tgt_ref[...] == me, len_ref[...], 0).astype(F32).astype(BF)
     sizes = nt(jnp.ones((8, NDP), BF), sent_here)
@@ -211,7 +217,6 @@
         sel[rows, :] = one_hot(bal_row[0:1, :] == here)
 
     loads[4].wait()
-    ag_step(1)
 
     def model_cols(rel):
         owner = lax.rem(z + rel, NT)
@@ -257,8 +262,8 @@
             toward[way],
         )
 
-    def rs_step(step, late=False):
-        for half in (0, 1):
+    def rs_step(step):
+        for half in (1, 0):
             for way in (0, 1):
                 order = half if way == 0 else 1 - half
                 rel = 4 - step if way == 0 else 4 + step
@@ -280,26 +285,78 @@
         both = pl.ds(2 * owner, 2)
         return remote(wp.at[1, both], sx.at[both], x_send.at[rel], x_recv.at[rel], sibling)
 
-    def weight_copy(m, slot):
-        return remote(
-            wp.at[0, m], wr.at[slot], w_send.at[m], w_recv.at[slot], {"dp": 2 * m + core}
-        )
-
-    def weight_send(rel):
+    def weight_sum(rel):
         owner, _ = model_cols(rel)
         sibling_copy(rel).wait_recv()
         for j in range(2):
             m = 2 * owner + j
             total = (wp[0, m].astype(F32) + sx[m].astype(F32)).astype(BF)
-            wp[0, m] = total
-
-            @pl.when(m != chip)
-            def _():
-                weight_copy(m, chip).start()
-
-            @pl.when(m == chip)
-            def _():
-                wr[m] = total
+            wsum[0, lax.rem(m, 4) * 4 + lax.div(m, 4)] = total[:HALF]
+            wsum[1, m] = total[HALF:]
+
+    col_of, row_of = lax.rem(chip, 4), lax.div(chip, 4)
+
+    def chip_ring(stage, part_of):
+        along_x = stage == part_of
+        at = col_of if along_x else row_of
+
+        def spot(k):
+            there = lax.rem(at + k, 4)
+            number = row_of * 4 + there if along_x else there * 4 + col_of
+            return {"dp": 2 * number + core}
+
+        def piece_of(k, high):
+            bundle = lax.rem(at + k, 4)
+            if stage == 0:
+                return (part_of, pl.ds(4 * bundle + 2 * high, 2))
+            return (part_of, bundle, pl.ds(128 * high, 128))
+
+        def near_of(way, high):
+            return (part_of, way, pl.ds(2 * high, 2) if stage == 0 else pl.ds(128 * high, 128))
+
+        source, far, near = (wsum, wfar, wnear) if stage == 0 else (vsum, vfar, vnear)
+
+        def copy(number):
+            way = number % 2
+            if number < 2:
+                src, dst = piece_of(2, way), (part_of, way)
+            else:
+                high = 1 - way if number < 4 else way
+                src, dst = piece_of(1 if way == 0 else 3, high), near_of(way, high)
+            return remote(
+                source.at[src],
+                far.at[dst] if number < 2 else near.at[dst],
+                w_send.at[stage, part_of, number],
+                w_recv.at[stage, part_of, number],
+                spot(1 if way == 0 else 3),
+            )
+
+        def begin():
+            for number in range(4):
+                copy(number).start()
+
+        def pass_on():
+            for way in (0, 1):
+                copy(way).wait_recv()
+                where = piece_of(1 if way == 0 else 3, way)
+                total = source[where].astype(F32) + far[part_of, way].astype(F32)
+                source[where] = total.astype(BF)
+                copy(4 + way).start()
+
+        def finish():
+            for number in range(2, 6):
+                copy(number).wait_recv()
+            own = (part_of, pl.ds(4 * at, 4)) if stage == 0 else (part_of, at)
+            total = source[own].astype(F32) + near[part_of, 0].astype(F32)
+            return total + near[part_of, 1].astype(F32)
+
+        def drain():
+            for number in range(6):
+                copy(number).wait_send()
+
+        return begin, pass_on, finish, drain
+
+    rings = [[chip_ring(stage, part_of) for part_of in (0, 1)] for stage in (0, 1)]
 
     project(4)
     rs_copy(0, 0, 0).start()
@@ -316,7 +373,7 @@
         weight_block(rel)
         sibling_copy(rel).start()
     for rel in (0, 1, 7):
-        weight_send(rel)
+        weight_sum(rel)
     ag_copy(0, 3, 0).wait_recv()
     ag_copy(1, 3, 1).wait_recv()
     rs_copy(0, 1, 1).start()
@@ -330,60 +387,69 @@
         sibling_copy(rel).start()
     project(2)
     project(6)
-    for rel in (2, 6):
-        weight_send(rel)
+    for rel in (2, 6, 3, 5, 4):
+        weight_sum(rel)
+    for ring in rings[0]:
+        ring[0]()
     rs_step(2)
     project(1)
     project(7)
-    for rel in (3, 5, 4):
-        weight_send(rel)
     project(0)
+    for ring in rings[0]:
+        ring[1]()
+    rs_step(3)
     exchange_wait(d_send, d_recv, d_ssem, d_rsem)
 
-    def backward(low, high):
-        @pl.loop(low, high)
-        def _(i):
-            rows = pl.ds(pl.multiple_of(i * TILE, TILE), TILE)
-            weights = probs[i]
-            half = weights.astype(BF)
-            dcontext = heads(d_recv, rows)
-            dweights = nt(pieces[rows, QC + HD : XC], dcontext)
-            delta = jnp.sum(half.astype(F32) * dweights, axis=0, keepdims=True)
-            dscores = (weights * (dweights - delta) * SCALE).astype(BF)
-            dq = tn(dscores, pieces[rows, QC : QC + HD]).astype(BF)
-            for h in range(GROUP):
-                gp[rows, h * HD : (h + 1) * HD] = dq[h * TILE : (h + 1) * TILE]
-            gp[rows, QC : QC + HD] = nn(dscores, heads(pieces, rows)).astype(BF)
-            gp[rows, QC + HD : XC] = nn(half, dcontext).astype(BF)
-
-    backward(0, 4)
-    rs_step(3)
-    backward(4, 8)
+    def backward(i):
+        rows = pl.ds(pl.multiple_of(i * TILE, TILE), TILE)
+        weights = probs[i]
+        half = weights.astype(BF)
+        dcontext = heads(d_recv, rows)
+        dweights = nt(pieces[rows, QC + HD : XC], dcontext)
+        delta = jnp.sum(half.astype(F32) * dweights, axis=0, keepdims=True)
+        dscores = (weights * (dweights - delta) * SCALE).astype(BF)
+        dq = tn(dscores, pieces[rows, QC : QC + HD]).astype(BF)
+        for h in range(GROUP):
+            gp[rows, h * HD : (h + 1) * HD] = dq[h * TILE : (h + 1) * TILE]
+        gp[rows, QC : QC + HD] = nn(dscores, heads(pieces, rows)).astype(BF)
+        gp[rows, QC + HD : XC] = nn(half, dcontext).astype(BF)
+
+    pl.loop(0, 4)(backward)
+    for half, ring in enumerate(rings[0]):
+        vsum[half] = ring[2]().astype(BF)
+    for ring in rings[1]:
+        ring[0]()
+    pl.loop(4, 8)(backward)
+    for ring in rings[1]:
+        ring[1]()
 
     @pl.loop(0, QC // 256)
     def _(i):
         cols = pl.ds(pl.multiple_of(i * 256, 256), 256)
-        gq_ref[:, cols] = nn(perm_t[...], gp[:, cols]).astype(BF)
+        gq[:, cols] = nn(perm_t[...], gp[:, cols]).astype(BF)
 
     both = nn(perm_t[...], gp[:, QC:XC]).astype(BF)
-    gk_ref[...] = both[:, :HD]
-    gv_ref[...] = both[:, HD:]
-
-    @pl.loop(1, NCHIP)
-    def _(k):
-        m = lax.rem(chip + k, NCHIP)
-        weight_copy(m, m).wait()
-
-    total = wr[0].astype(F32)
-    for m in range(1, NCHIP):
-        total = total + wr[m].astype(F32)
-    wg_ref[...] = total
+    gk[...] = both[:, :HD]
+    gv[...] = both[:, HD:]
+    stores = [
+        pltpu.make_async_copy(src, dst, store_sem.at[i])
+        for i, (src, dst) in enumerate(
+            ((gq, gq_out), (gk, gk_out), (gv, gv_out), (wg, wg_out), (lo, lo_out))
+        )
+    ]
+    for one in stores[:3]:
+        one.start()
+
+    for half, ring in enumerate(rings[1]):
+        wg[half * HALF : (half + 1) * HALF, :] = ring[2]()
+    stores[3].start()
 
     for way in (0, 1):
         for half in (0, 1):
             rs_copy(way, 3, half).wait_recv()
     total = part[0].astype(F32) + rs_recv[0, 3].astype(F32) + rs_recv[1, 3].astype(F32)
-    lo_ref[...] = total.astype(BF)
+    lo[...] = total.astype(BF)
+    stores[4].start()
 
     for way in (0, 1):
         for step in range(4):
@@ -394,6 +460,23 @@
                     rs_copy(way, step, half).wait_send()
     for rel in range(NT):
         sibling_copy(rel).wait_send()
+    for ring in rings[0] + rings[1]:
+        ring[3]()
+    for one in stores:
+        one.wait()
+
+
+def hand_over(*refs):
+    sources, dests, stage, sems = refs[:5], refs[5:10], refs[10:15], refs[15]
+    loads = [pltpu.make_async_copy(sources[i], stage[i], sems.at[0, i]) for i in range(5)]
+    stores = [pltpu.make_async_copy(stage[i], dests[i], sems.at[1, i]) for i in range(5)]
+    for one in loads:
+        one.start()
+    for load, store in zip(loads, stores):
+        load.wait()
+        store.start()
+    for one in stores:
+        one.wait()
 
 
 def shards(query_rows, key_rows, value_rows, out_grad, w_out, lengths, target):
@@ -431,10 +514,20 @@
         pltpu.VMEM((CAP, QC), F32),
         pltpu.VMEM((2, NCHIP, QC, 128), BF),
         pltpu.VMEM((NCHIP, QC, 128), BF),
-        pltpu.VMEM((NCHIP, QC, 128), BF),
+        pltpu.VMEM((2, NCHIP, HALF, 128), BF),
+        pltpu.VMEM((2, 2, 2, HALF, 128), BF),
+        pltpu.VMEM((2, 2, 4, HALF, 128), BF),
+        pltpu.VMEM((2, 4, HALF, 128), BF),
+        pltpu.VMEM((2, 2, 128, 128), BF),
+        pltpu.VMEM((2, 2, HALF, 128), BF),
         pltpu.VMEM((PACK, QC), BF),
         pltpu.VMEM((PACK, QC), BF),
         pltpu.VMEM((PACK, XC), BF),
+        pltpu.VMEM((CAP, MC), BF),
+        pltpu.VMEM((PACK, QC), BF),
+        pltpu.VMEM((PACK, HD), BF),
+        pltpu.VMEM((PACK, HD), BF),
+        pltpu.VMEM((QC, 128), F32),
         dma((5,)),
         dma((2, 4, 2)),
         dma((2, 4, 2)),
@@ -446,19 +539,27 @@
         dma((NDP,)),
         dma((NT,)),
         dma((NT,)),
-        dma((NCHIP,)),
-        dma((NCHIP,)),
+        dma((2, 2, 6)),
+        dma((2, 2, 6)),
+        dma((5,)),
     ]
-    return pl.pallas_call(
+    results = pl.pallas_call(
         kernel,
         out_shape=outs,
         in_specs=[hbm, hbm, hbm, hbm, hbm, vmem, vmem],
-        out_specs=(vmem,) * 5,
+        out_specs=(hbm,) * 5,
         scratch_shapes=scratch,
         compiler_params=pltpu.CompilerParams(
             collective_id=0, has_side_effects=True, vmem_limit_bytes=60 * 2**20
         ),
     )(query_rows, key_rows, value_rows, out_grad, w_out, lengths, target)
+    return pl.pallas_call(
+        hand_over,
+        out_shape=outs,
+        in_specs=[hbm] * 5,
+        out_specs=(hbm,) * 5,
+        scratch_shapes=[pltpu.VMEM(o.shape, o.dtype) for o in outs] + [dma((2, 5))],
+    )(*results)
 
 
 def solution(mesh):

time: 120 us -> 101 us (0.84)
  Pallas kernels: 111 us -> 99.7 us
  local copies, waits for them, and re-layouts: 8.22 us -> 0 us
    pallas_call x1, Pallas kernels: 111 us -> 97 us  [shards(): pl.pallas_call(kernel, out_shape=outs, in_specs=[hbm, hbm, hbm, hbm, hbm,...]
    unnamed x7 -> x0, local copies, waits for them, and re-layouts: 8.22 us -> none
    pallas_call x0 -> x1, Pallas kernels: none -> 2.7 us  [shards(): pl.pallas_call(hand_over, out_shape=outs, in_specs=[hbm] * 5, out_specs=(...]
where the time goes in v3:
time: 101 us; the launch traced here: 100 us
  Pallas kernels  99.7 us (99%)
    pallas_call x1, Pallas kernels, shards(): pl.pallas_call(kernel, out_shape=outs, in_specs=[hbm, hbm, hbm, hbm, hbm,...  97 us
    pallas_call x1, Pallas kernels, shards(): pl.pallas_call(hand_over, out_shape=outs, in_specs=[hbm] * 5, out_specs=(...  2.7 us

profile of v3, /device:TPU:1, one launch (start us, length us, event | category | flops | bytes accessed | tf_op | source)
XLA Modules:
  0.0 100.3 jit_solution(13122631626221448786)
XLA Ops:
  0.6 97.0 %shard_map.110 = (bf16[512,512]{1,0:T(8,128)(2,1)}, bf16[1024,512]{1,0:T(8,128)(2,1)}, bf16[1024,128]{1,0:T(8,128)(2,1)}, bf16[1024,128]{1,0:T(8,128)(2,1)}, f32[512,128]{1,0:T(8,128)}) custom-call(bf16[1024,512]{1,0:T(8,128)(2,1)} %q_in.1, bf16[1024,128]{1,0:T(8,128)(2,1)} %k_in.1, bf16[1024,128]{1,0:T(8,128)(2,1)} %v_in.1, bf16[512,512]{1,0:T(8,128)(2,1)} %og_in.1, ...), custom_call_target="tpu_custom_call" | custom-call | tf_op jit(solution)/shard_map/pallas_call | solution.py:546
  97.6 2.7 %shard_map.111 = (bf16[512,512]{1,0:T(8,128)(2,1)}, bf16[1024,512]{1,0:T(8,128)(2,1)}, bf16[1024,128]{1,0:T(8,128)(2,1)}, bf16[1024,128]{1,0:T(8,128)(2,1)}, f32[512,128]{1,0:T(8,128)}) custom-call(bf16[512,512]{1,0:T(8,128)(2,1)} %get-tuple-element.10.refs_0_, bf16[1024,512]{1,0:T(8,128)(2,1)} %get-tuple-element.11.refs_1_, ...), custom_call_target="tpu_custom_call" | custom-call | tf_op jit(solution)/shard_map/pallas_call | solution.py:556

commit v4 on v3

--- a/solution.py
+++ b/solution.py
@@ -70,10 +70,10 @@
     q_in, k_in, v_in, og_in, w_in, len_ref, tgt_ref,
     lo_out, gq_out, gk_out, gv_out, wg_out,
     home, pieces, og, w, perm, perm_t, sel, sel_t, home_col, home_row, bal_col, bal_row, bias, probs,
-    ctx_send, ctx_recv, bctx, bctx_t, part, rs_recv, dbal, wp, sx, wsum, wfar, wnear, vsum, vfar, vnear,
+    ctx_send, ctx_recv, bctx, bctx_t, p_end, p_mid, c_out, r_in, r_out, r_own, wx, dbal, wp, sx, wsum, wfar, wnear, vsum, vfar, vnear,
     d_send, d_recv, gp,
     lo, gq, gk, gv, wg,
-    load_sem, ag_send, ag_recv, rs_send, rs_recv_sem, c_send, c_recv, d_ssem, d_rsem,
+    load_sem, ag_send, ag_recv, rs_send, rs_recv, wz_send, wz_recv, wa_send, wa_recv, c_send, c_recv, d_ssem, d_rsem,
     x_send, x_recv, w_send, w_recv, store_sem,
 ):
     me = lax.axis_index("dp")
@@ -83,6 +83,12 @@
     right, left = {"tensor": lax.rem(z + 1, NT)}, {"tensor": lax.rem(z + NT - 1, NT)}
     toward = (right, left)
     sibling = {"dp": me + 1 - 2 * core}
+    col_of, row_of = lax.rem(chip, 4), lax.div(chip, 4)
+
+    sign = 1 - 2 * lax.rem(z, 2)
+
+    def plane(k):
+        return lax.rem(z + sign * k + 2 * NT, NT)
 
     loads = [
         pltpu.make_async_copy(q_in, home.at[:, pl.ds(0, QC)], load_sem.at[0]),
@@ -97,6 +103,10 @@
     barrier = pltpu.get_barrier_semaphore()
     pl.semaphore_signal(barrier, inc=1, device_id=right, device_id_type=MESH)
     pl.semaphore_signal(barrier, inc=1, device_id=left, device_id_type=MESH)
+    for k in (2, NT - 2):
+        pl.semaphore_signal(
+            barrier, inc=1, device_id={"tensor": lax.rem(z + k, NT)}, device_id_type=MESH
+        )
 
     @pl.loop(1, NDP)
     def _(k):
@@ -104,7 +114,7 @@
             barrier, inc=1, device_id={"dp": lax.rem(me + k, NDP)}, device_id_type=MESH
         )
 
-    pl.semaphore_wait(barrier, NDP + 1)
+    pl.semaphore_wait(barrier, NDP + 3)
 
     halves = (pl.ds(0, HALF), pl.ds(HALF, HALF))
 
@@ -131,6 +141,66 @@
                 if order in ag_halves(way, step):
                     ag_copy(way, step, order).start()
 
+    def wz_copy(i, j):
+        a, b = (col_of, row_of) if i == 0 else (row_of, col_of)
+        rows = pl.ds(pl.multiple_of(256 * core + 64 * b + 16 * a, 16), 16)
+        cols = pl.ds(pl.multiple_of(plane(-1 - j if i == 0 else 2 + j) * MC, MC), MC)
+        return remote(
+            w_in.at[rows, cols],
+            wx.at[i, j, rows],
+            wz_send.at[i, j],
+            wz_recv.at[i, j],
+            {"tensor": plane(-1 if i == 0 else 2)},
+        )
+
+    def chip_at(along_x, k):
+        there = lax.rem((col_of if along_x else row_of) + k, 4)
+        number = row_of * 4 + there if along_x else there * 4 + col_of
+        return {"dp": 2 * number + core}
+
+    def wa_copy(i, stage, number):
+        a, b = (col_of, row_of) if i == 0 else (row_of, col_of)
+        along_x = (i == 0) == (stage == 0)
+        way = number % 2
+        step = 0 if number < 2 else 3 if way == 0 else 1
+        if stage == 0:
+            start = 256 * core + 64 * b + 16 * lax.rem(a + step, 4)
+            rows = pl.ds(pl.multiple_of(start, 16), 16)
+        else:
+            rows = pl.ds(pl.multiple_of(256 * core + 64 * lax.rem(b + step, 4), 64), 64)
+        blocks = pl.ds(0, 4) if number < 2 else pl.ds(2 * way, 2)
+        ref = wx.at[i, blocks, rows]
+        return remote(
+            ref,
+            ref,
+            wa_send.at[i, stage, number],
+            wa_recv.at[i, stage, number],
+            chip_at(along_x, 1 if way == 0 else 3),
+        )
+
+    def wx_sibling(i):
+        ref = wx.at[i, :, pl.ds(pl.multiple_of(256 * core, 256), 256)]
+        return remote(ref, ref, wa_send.at[i, 2, 0], wa_recv.at[i, 2, 0], sibling)
+
+    def wx_step(step):
+        for i in (0, 1):
+            if step == 0:
+                for j in range(4):
+                    wz_copy(i, j).wait_recv()
+            elif step < 5:
+                for way in (0, 1):
+                    wa_copy(i, (step - 1) // 2, way + 2 * ((step - 1) % 2)).wait_recv()
+            else:
+                wx_sibling(i).wait_recv()
+            if step < 4:
+                for way in (0, 1):
+                    wa_copy(i, step // 2, way + 2 * (step % 2)).start()
+            elif step == 4:
+                wx_sibling(i).start()
+
+    for j in range(4):
+        for i in (0, 1):
+            wz_copy(i, j).start()
     loads[3].wait()
     ag_step(0)
 
@@ -156,6 +226,8 @@
     def _(i):
         cols = pl.ds(pl.multiple_of(i * 256, 256), 256)
         pieces[:, cols] = nn(perm[...], home[:, cols]).astype(BF)
+
+    wx_step(0)
 
     key_row = iota((TILE, QC), 0)
     query_row = iota((TILE, QC), 1) % TILE
@@ -175,12 +247,26 @@
         for h in range(GROUP):
             ctx_send[rows, h * HD : (h + 1) * HD] = context[h * TILE : (h + 1) * TILE]
 
-    pl.loop(0, 4)(forward)
-    ag_step(1, (0,))
-    pl.loop(4, 8)(forward)
-
     def piece(d):
         return pl.ds(pl.multiple_of(d * SLOT, SLOT), SLOT)
+
+    def forward_and_send(i):
+        tile = lax.rem(lax.div(me, 4) + i, PACK // TILE)
+        forward(tile)
+        for j in range(4):
+            d = 4 * tile + j
+
+            @pl.when(d != me)
+            def _():
+                remote(
+                    ctx_send.at[piece(d)], ctx_recv.at[piece(me)], c_send.at[d], c_recv.at[me], {"dp": d}
+                ).start()
+
+    pl.loop(0, 4)(forward_and_send)
+    wx_step(1)
+    ag_step(1, (0,))
+    pl.loop(4, 8)(forward_and_send)
+    ctx_recv[piece(me), :] = ctx_send[piece(me), :]
 
     def exchange_start(source, dest, send, recv):
         @pl.loop(1, NDP)
@@ -200,7 +286,6 @@
                 source.at[piece(d)], dest.at[piece(d)], send.at[d], recv.at[d], {"dp": d}
             ).wait()
 
-    exchange_start(ctx_send, ctx_recv, c_send, c_recv)
     ag_step(1, (1,))
 
     sent_here = jnp.where(tgt_ref[...] == me, len_ref[...], 0).astype(F32).astype(BF)
@@ -239,7 +324,9 @@
         index = bal_col[rows, 0:1]
         sel_t[rows, :] = one_hot(index == iota((TILE, CAP), 1).astype(F32))
 
+    wx_step(2)
     ag_step(2)
+    wx_step(3)
     add_dbalanced(2)
     add_dbalanced(6)
 
@@ -248,31 +335,40 @@
     bctx[...] = balanced
     bctx_t[...] = balanced.T
 
-    def project(rel):
-        _, cols = model_cols(rel)
-        part[rel] = nn(bctx[...], w[:, cols]).astype(BF)
-
-    def rs_copy(way, step, half):
-        rel = 4 - step if way == 0 else 4 + step
-        return remote(
-            part.at[rel, halves[half]],
-            rs_recv.at[way, step, halves[half]],
-            rs_send.at[way, step, half],
-            rs_recv_sem.at[way, step, half],
-            toward[way],
-        )
-
-    def rs_step(step):
-        for half in (1, 0):
-            for way in (0, 1):
-                order = half if way == 0 else 1 - half
-                rel = 4 - step if way == 0 else 4 + step
-                if order in ag_halves(way, 3 if step == 1 else 0):
-                    rs_copy(way, step - 1, order).wait_recv()
-                    rows = halves[order]
-                    total = part[rel, rows].astype(F32) + rs_recv[way, step - 1, rows].astype(F32)
-                    part[rel, rows] = total.astype(BF)
-                    rs_copy(way, step, order).start()
+    quarter = lax.rem(z, 4)
+    end = lax.rem(lax.div(quarter + 1, 2), 2)
+    end_rows = pl.ds(pl.multiple_of(end * HALF, HALF), HALF)
+    mid_rows = pl.ds(pl.multiple_of((1 - end) * HALF, HALF), HALF)
+    partner, other = {"tensor": plane(1)}, {"tensor": plane(-1)}
+
+    def plane_cols(k):
+        return pl.ds(pl.multiple_of(plane(k) * MC, MC), MC)
+
+    def rs_copy(number):
+        src, dst, where = (
+            (bctx.at[end_rows], c_out.at[0], other),
+            (bctx.at[mid_rows], c_out.at[1], {"tensor": plane(2)}),
+            (p_end.at[1], r_in.at[0], partner),
+            (p_end.at[2], r_in.at[1], partner),
+            (p_end.at[3], r_in.at[2], partner),
+            (p_mid.at[2], r_out.at[0], other),
+            (p_mid.at[3], r_out.at[1], other),
+            (p_mid.at[1], r_own, partner),
+        )[number]
+        return remote(src, dst, rs_send.at[number], rs_recv.at[number], where)
+
+    def project_mid():
+        for slot, k in enumerate((0, 1, -1, -2)):
+            p_mid[slot] = nn(bctx[mid_rows, :], w[:, plane_cols(k)]).astype(BF)
+
+    def project_end(k):
+        total = nn(bctx[end_rows, :], w[:, plane_cols(k)])
+        total = total + nn(c_out[0], wx[0, k]) + nn(c_out[1], wx[1, k])
+        p_end[k] = total.astype(BF)
+
+    def pass_on(slot, ref, number):
+        p_mid[slot] = (p_mid[slot].astype(F32) + ref[...].astype(F32)).astype(BF)
+        rs_copy(number).start()
 
     def weight_block(rel):
         owner, _ = model_cols(rel)
@@ -294,16 +390,9 @@
             wsum[0, lax.rem(m, 4) * 4 + lax.div(m, 4)] = total[:HALF]
             wsum[1, m] = total[HALF:]
 
-    col_of, row_of = lax.rem(chip, 4), lax.div(chip, 4)
-
     def chip_ring(stage, part_of):
         along_x = stage == part_of
         at = col_of if along_x else row_of
-
-        def spot(k):
-            there = lax.rem(at + k, 4)
-            number = row_of * 4 + there if along_x else there * 4 + col_of
-            return {"dp": 2 * number + core}
 
         def piece_of(k, high):
             bundle = lax.rem(at + k, 4)
@@ -328,7 +417,7 @@
                 far.at[dst] if number < 2 else near.at[dst],
                 w_send.at[stage, part_of, number],
                 w_recv.at[stage, part_of, number],
-                spot(1 if way == 0 else 3),
+                chip_at(along_x, 1 if way == 0 else 3),
             )
 
         def begin():
@@ -358,15 +447,14 @@
 
     rings = [[chip_ring(stage, part_of) for part_of in (0, 1)] for stage in (0, 1)]
 
-    project(4)
-    rs_copy(0, 0, 0).start()
-    rs_copy(1, 0, 1).start()
+    wx_step(4)
+    project_mid()
     for rel in (0, 1, 7):
         weight_block(rel)
         sibling_copy(rel).start()
     ag_step(3)
-    project(3)
-    project(5)
+    rs_copy(1).start()
+    rs_copy(0).start()
     add_dbalanced(3)
     add_dbalanced(5)
     for rel in (2, 6):
@@ -376,33 +464,45 @@
         weight_sum(rel)
     ag_copy(0, 3, 0).wait_recv()
     ag_copy(1, 3, 1).wait_recv()
-    rs_copy(0, 1, 1).start()
-    rs_copy(1, 1, 0).start()
     add_dbalanced(4)
     d_send[...] = nn(sel_t[...], dbal[...].astype(BF)).astype(BF)
     exchange_start(d_send, d_recv, d_ssem, d_rsem)
-    rs_step(1)
+    wx_step(5)
+    rs_copy(0).wait_recv()
+    rs_copy(1).wait_recv()
+    for k in (3, 2, 1):
+        project_end(k)
+        rs_copy(1 + k).start()
     for rel in (3, 5, 4):
         weight_block(rel)
         sibling_copy(rel).start()
-    project(2)
-    project(6)
+    project_end(0)
     for rel in (2, 6, 3, 5, 4):
         weight_sum(rel)
     for ring in rings[0]:
         ring[0]()
-    rs_step(2)
-    project(1)
-    project(7)
-    project(0)
+    rs_copy(4).wait_recv()
+    pass_on(3, r_in.at[2], 6)
     for ring in rings[0]:
         ring[1]()
-    rs_step(3)
-    exchange_wait(d_send, d_recv, d_ssem, d_rsem)
+    rs_copy(3).wait_recv()
+    pass_on(2, r_in.at[1], 5)
+    rs_copy(6).wait_recv()
+    pass_on(1, r_out.at[1], 7)
 
     def backward(i):
-        rows = pl.ds(pl.multiple_of(i * TILE, TILE), TILE)
-        weights = probs[i]
+        tile = lax.rem(lax.div(me, 4) + 8 - i, PACK // TILE)
+        for j in range(4):
+            d = 4 * tile + j
+
+            @pl.when(d != me)
+            def _():
+                remote(
+                    d_send.at[piece(d)], d_recv.at[piece(d)], d_ssem.at[d], d_rsem.at[d], {"dp": d}
+                ).wait()
+
+        rows = pl.ds(pl.multiple_of(tile * TILE, TILE), TILE)
+        weights = probs[tile]
         half = weights.astype(BF)
         dcontext = heads(d_recv, rows)
         dweights = nt(pieces[rows, QC + HD : XC], dcontext)
@@ -444,11 +544,13 @@
         wg[half * HALF : (half + 1) * HALF, :] = ring[2]()
     stores[3].start()
 
-    for way in (0, 1):
-        for half in (0, 1):
-            rs_copy(way, 3, half).wait_recv()
-    total = part[0].astype(F32) + rs_recv[0, 3].astype(F32) + rs_recv[1, 3].astype(F32)
-    lo[...] = total.astype(BF)
+    for number in (2, 5):
+        rs_copy(number).wait_recv()
+    total = p_mid[0].astype(F32) + r_in[0].astype(F32) + r_out[0].astype(F32)
+    lo[mid_rows, :] = total.astype(BF)
+    rs_copy(7).wait_recv()
+    total = p_end[0].astype(F32) + r_own[...].astype(F32)
+    lo[end_rows, :] = total.astype(BF)
     stores[4].start()
 
     for way in (0, 1):
@@ -456,8 +558,14 @@
             for half in (0, 1):
                 if half in ag_halves(way, step):
                     ag_copy(way, step, half).wait_send()
-                if half in ag_halves(way, 3 - step):
-                    rs_copy(way, step, half).wait_send()
+    for number in range(8):
+        rs_copy(number).wait_send()
+    for i in (0, 1):
+        for j in range(4):
+            wz_copy(i, j).wait_send()
+            wa_copy(i, 0, j).wait_send()
+            wa_copy(i, 1, j).wait_send()
+        wx_sibling(i).wait_send()
     for rel in range(NT):
         sibling_copy(rel).wait_send()
     for ring in rings[0] + rings[1]:
@@ -509,8 +617,13 @@
         pltpu.VMEM((PACK, QC), BF),
         pltpu.VMEM((CAP, QC), BF),
         pltpu.VMEM((QC, CAP), BF),
-        pltpu.VMEM((NT, CAP, MC), BF),
-        pltpu.VMEM((2, 4, CAP, MC), BF),
+        pltpu.VMEM((4, HALF, MC), BF),
+        pltpu.VMEM((4, HALF, MC), BF),
+        pltpu.VMEM((2, HALF, QC), BF),
+        pltpu.VMEM((3, HALF, MC), BF),
+        pltpu.VMEM((2, HALF, MC), BF),
+        pltpu.VMEM((HALF, MC), BF),
+        pltpu.VMEM((2, 4, QC, MC), BF),
         pltpu.VMEM((CAP, QC), F32),
         pltpu.VMEM((2, NCHIP, QC, 128), BF),
         pltpu.VMEM((NCHIP, QC, 128), BF),
@@ -531,8 +644,12 @@
         dma((5,)),
         dma((2, 4, 2)),
         dma((2, 4, 2)),
-        dma((2, 4, 2)),
-        dma((2, 4, 2)),
+        dma((8,)),
+        dma((8,)),
+        dma((2, 4)),
+        dma((2, 4)),
+        dma((2, 3, 4)),
+        dma((2, 3, 4)),
         dma((NDP,)),
         dma((NDP,)),
         dma((NDP,)),

time: 101 us -> 98.4 us (0.974); the launches traced: 100 us -> 96.5 us
  Pallas kernels: 99.7 us -> 95.9 us
    pallas_call x1, Pallas kernels: 97 us -> 93.2 us  [shards(): pl.pallas_call(kernel, out_shape=outs, in_specs=[hbm, hbm, hbm, hbm, hbm,...]
where the time goes in v4:
time: 98.4 us; the launch traced here: 96.5 us
  Pallas kernels  95.9 us (97%)
    pallas_call x1, Pallas kernels, shards(): pl.pallas_call(kernel, out_shape=outs, in_specs=[hbm, hbm, hbm, hbm, hbm,...  93.2 us
    pallas_call x1, Pallas kernels, shards(): pl.pallas_call(hand_over, out_shape=outs, in_specs=[hbm] * 5, out_specs=(...  2.7 us

profile of v4, /device:TPU:1, one launch (start us, length us, event | category | flops | bytes accessed | tf_op | source)
XLA Modules:
  0.0 96.5 jit_solution(4771925518072943129)
XLA Ops:
  0.6 93.2 %shard_map.110 = (bf16[512,512]{1,0:T(8,128)(2,1)}, bf16[1024,512]{1,0:T(8,128)(2,1)}, bf16[1024,128]{1,0:T(8,128)(2,1)}, bf16[1024,128]{1,0:T(8,128)(2,1)}, f32[512,128]{1,0:T(8,128)}) custom-call(bf16[1024,512]{1,0:T(8,128)(2,1)} %q_in.1, bf16[1024,128]{1,0:T(8,128)(2,1)} %k_in.1, bf16[1024,128]{1,0:T(8,128)(2,1)} %v_in.1, bf16[512,512]{1,0:T(8,128)(2,1)} %og_in.1, ...), custom_call_target="tpu_custom_call" | custom-call | tf_op jit(solution)/shard_map/pallas_call | solution.py:663
  93.8 2.7 %shard_map.111 = (bf16[512,512]{1,0:T(8,128)(2,1)}, bf16[1024,512]{1,0:T(8,128)(2,1)}, bf16[1024,128]{1,0:T(8,128)(2,1)}, bf16[1024,128]{1,0:T(8,128)(2,1)}, f32[512,128]{1,0:T(8,128)}) custom-call(bf16[512,512]{1,0:T(8,128)(2,1)} %get-tuple-element.10.refs_0_, bf16[1024,512]{1,0:T(8,128)(2,1)} %get-tuple-element.11.refs_1_, ...), custom_call_target="tpu_custom_call" | custom-call | tf_op jit(solution)/shard_map/pallas_call | solution.py:673

commit v5 on v4

--- a/solution.py
+++ b/solution.py
@@ -337,38 +337,48 @@
 
     quarter = lax.rem(z, 4)
     end = lax.rem(lax.div(quarter + 1, 2), 2)
-    end_rows = pl.ds(pl.multiple_of(end * HALF, HALF), HALF)
-    mid_rows = pl.ds(pl.multiple_of((1 - end) * HALF, HALF), HALF)
+    mid = 1 - end
+    halves_of = (pl.ds(0, TILE), pl.ds(TILE, TILE))
+
+    def rows_at(half, sub):
+        return pl.ds(pl.multiple_of(half * HALF + sub * TILE, TILE), TILE)
+
     partner, other = {"tensor": plane(1)}, {"tensor": plane(-1)}
 
     def plane_cols(k):
         return pl.ds(pl.multiple_of(plane(k) * MC, MC), MC)
 
-    def rs_copy(number):
+    def rs_copy(number, sub):
+        rows = halves_of[sub]
         src, dst, where = (
-            (bctx.at[end_rows], c_out.at[0], other),
-            (bctx.at[mid_rows], c_out.at[1], {"tensor": plane(2)}),
-            (p_end.at[1], r_in.at[0], partner),
-            (p_end.at[2], r_in.at[1], partner),
-            (p_end.at[3], r_in.at[2], partner),
-            (p_mid.at[2], r_out.at[0], other),
-            (p_mid.at[3], r_out.at[1], other),
-            (p_mid.at[1], r_own, partner),
+            (bctx.at[rows_at(end, sub)], c_out.at[0, rows], other),
+            (bctx.at[rows_at(mid, sub)], c_out.at[1, rows], {"tensor": plane(2)}),
+            (p_end.at[1, rows], r_in.at[0, rows], partner),
+            (p_end.at[2, rows], r_in.at[1, rows], partner),
+            (p_end.at[3, rows], r_in.at[2, rows], partner),
+            (p_mid.at[2, rows], r_out.at[0, rows], other),
+            (p_mid.at[3, rows], r_out.at[1, rows], other),
+            (p_mid.at[1, rows], r_own.at[rows], partner),
         )[number]
-        return remote(src, dst, rs_send.at[number], rs_recv.at[number], where)
+        return remote(src, dst, rs_send.at[number, sub], rs_recv.at[number, sub], where)
 
     def project_mid():
+        rows = pl.ds(pl.multiple_of(mid * HALF, HALF), HALF)
         for slot, k in enumerate((0, 1, -1, -2)):
-            p_mid[slot] = nn(bctx[mid_rows, :], w[:, plane_cols(k)]).astype(BF)
-
-    def project_end(k):
-        total = nn(bctx[end_rows, :], w[:, plane_cols(k)])
-        total = total + nn(c_out[0], wx[0, k]) + nn(c_out[1], wx[1, k])
-        p_end[k] = total.astype(BF)
-
-    def pass_on(slot, ref, number):
-        p_mid[slot] = (p_mid[slot].astype(F32) + ref[...].astype(F32)).astype(BF)
-        rs_copy(number).start()
+            p_mid[slot] = nn(bctx[rows, :], w[:, plane_cols(k)]).astype(BF)
+
+    def project_end(k, sub):
+        rows = halves_of[sub]
+        total = nn(bctx[rows_at(end, sub), :], w[:, plane_cols(k)])
+        total = total + nn(c_out[0, rows], wx[0, k]) + nn(c_out[1, rows], wx[1, k])
+        p_end[k, rows] = total.astype(BF)
+
+    def pass_on(slot, ref, number, arrival):
+        for sub, rows in enumerate(halves_of):
+            rs_copy(arrival, sub).wait_recv()
+            total = p_mid[slot, rows].astype(F32) + ref[rows].astype(F32)
+            p_mid[slot, rows] = total.astype(BF)
+            rs_copy(number, sub).start()
 
     def weight_block(rel):
         owner, _ = model_cols(rel)
@@ -453,42 +463,39 @@
         weight_block(rel)
         sibling_copy(rel).start()
     ag_step(3)
-    rs_copy(1).start()
-    rs_copy(0).start()
+    for sub in (0, 1):
+        rs_copy(1, sub).start()
+        rs_copy(0, sub).start()
     add_dbalanced(3)
     add_dbalanced(5)
-    for rel in (2, 6):
+    for rel in (2, 6, 3, 5):
         weight_block(rel)
         sibling_copy(rel).start()
-    for rel in (0, 1, 7):
+    for rel in (0, 1, 7, 2, 6, 3, 5):
         weight_sum(rel)
     ag_copy(0, 3, 0).wait_recv()
     ag_copy(1, 3, 1).wait_recv()
     add_dbalanced(4)
     d_send[...] = nn(sel_t[...], dbal[...].astype(BF)).astype(BF)
     exchange_start(d_send, d_recv, d_ssem, d_rsem)
+    weight_block(4)
+    sibling_copy(4).start()
     wx_step(5)
-    rs_copy(0).wait_recv()
-    rs_copy(1).wait_recv()
-    for k in (3, 2, 1):
-        project_end(k)
-        rs_copy(1 + k).start()
-    for rel in (3, 5, 4):
-        weight_block(rel)
-        sibling_copy(rel).start()
-    project_end(0)
-    for rel in (2, 6, 3, 5, 4):
-        weight_sum(rel)
+    weight_sum(4)
     for ring in rings[0]:
         ring[0]()
-    rs_copy(4).wait_recv()
-    pass_on(3, r_in.at[2], 6)
+    for sub in (0, 1):
+        rs_copy(0, sub).wait_recv()
+        rs_copy(1, sub).wait_recv()
+        for k in (3, 2, 1):
+            project_end(k, sub)
+            rs_copy(1 + k, sub).start()
+        project_end(0, sub)
+    pass_on(3, r_in.at[2], 6, 4)
     for ring in rings[0]:
         ring[1]()
-    rs_copy(3).wait_recv()
-    pass_on(2, r_in.at[1], 5)
-    rs_copy(6).wait_recv()
-    pass_on(1, r_out.at[1], 7)
+    pass_on(2, r_in.at[1], 5, 3)
+    pass_on(1, r_out.at[1], 7, 6)
 
     def backward(i):
         tile = lax.rem(lax.div(me, 4) + 8 - i, PACK // TILE)
@@ -544,13 +551,15 @@
         wg[half * HALF : (half + 1) * HALF, :] = ring[2]()
     stores[3].start()
 
-    for number in (2, 5):
-        rs_copy(number).wait_recv()
-    total = p_mid[0].astype(F32) + r_in[0].astype(F32) + r_out[0].astype(F32)
-    lo[mid_rows, :] = total.astype(BF)
-    rs_copy(7).wait_recv()
-    total = p_end[0].astype(F32) + r_own[...].astype(F32)
-    lo[end_rows, :] = total.astype(BF)
+    for sub, rows in enumerate(halves_of):
+        rs_copy(2, sub).wait_recv()
+        rs_copy(5, sub).wait_recv()
+        total = p_mid[0, rows].astype(F32) + r_in[0, rows].astype(F32)
+        lo[rows_at(mid, sub), :] = (total + r_out[0, rows].astype(F32)).astype(BF)
+    for sub, rows in enumerate(halves_of):
+        rs_copy(7, sub).wait_recv()
+        total = p_end[0, rows].astype(F32) + r_own[rows].astype(F32)
+        lo[rows_at(end, sub), :] = total.astype(BF)
     stores[4].start()
 
     for way in (0, 1):
@@ -559,7 +568,8 @@
                 if half in ag_halves(way, step):
                     ag_copy(way, step, half).wait_send()
     for number in range(8):
-        rs_copy(number).wait_send()
+        for sub in (0, 1):
+            rs_copy(number, sub).wait_send()
     for i in (0, 1):
         for j in range(4):
             wz_copy(i, j).wait_send()
@@ -644,8 +654,8 @@
         dma((5,)),
         dma((2, 4, 2)),
         dma((2, 4, 2)),
-        dma((8,)),
-        dma((8,)),
+        dma((8, 2)),
+        dma((8, 2)),
         dma((2, 4)),
         dma((2, 4)),
         dma((2, 3, 4)),

time: 98.4 us -> 102 us (1.037); the launches traced: 96.5 us -> 101 us
  Pallas kernels: 95.9 us -> 101 us
    pallas_call x1, Pallas kernels: 93.2 us -> 98 us  [shards(): pl.pallas_call(kernel, out_shape=outs, in_specs=[hbm, hbm, hbm, hbm, hbm,...]
where the time goes in v5:
time: 102 us; the launch traced here: 101 us
  Pallas kernels  101 us (99%)
    pallas_call x1, Pallas kernels, shards(): pl.pallas_call(kernel, out_shape=outs, in_specs=[hbm, hbm, hbm, hbm, hbm,...  98 us
    pallas_call x1, Pallas kernels, shards(): pl.pallas_call(hand_over, out_shape=outs, in_specs=[hbm] * 5, out_specs=(...  2.7 us

profile of v5, /device:TPU:1, one launch (start us, length us, event | category | flops | bytes accessed | tf_op | source)
XLA Modules:
  0.0 101.3 jit_solution(6813286317708167968)
XLA Ops:
  0.6 98.0 %shard_map.110 = (bf16[512,512]{1,0:T(8,128)(2,1)}, bf16[1024,512]{1,0:T(8,128)(2,1)}, bf16[1024,128]{1,0:T(8,128)(2,1)}, bf16[1024,128]{1,0:T(8,128)(2,1)}, f32[512,128]{1,0:T(8,128)}) custom-call(bf16[1024,512]{1,0:T(8,128)(2,1)} %q_in.1, bf16[1024,128]{1,0:T(8,128)(2,1)} %k_in.1, bf16[1024,128]{1,0:T(8,128)(2,1)} %v_in.1, bf16[512,512]{1,0:T(8,128)(2,1)} %og_in.1, ...), custom_call_target="tpu_custom_call" | custom-call | tf_op jit(solution)/shard_map/pallas_call | solution.py:673
  98.6 2.7 %shard_map.111 = (bf16[512,512]{1,0:T(8,128)(2,1)}, bf16[1024,512]{1,0:T(8,128)(2,1)}, bf16[1024,128]{1,0:T(8,128)(2,1)}, bf16[1024,128]{1,0:T(8,128)(2,1)}, f32[512,128]{1,0:T(8,128)}) custom-call(bf16[512,512]{1,0:T(8,128)(2,1)} %get-tuple-element.10.refs_0_, bf16[1024,512]{1,0:T(8,128)(2,1)} %get-tuple-element.11.refs_1_, ...), custom_call_target="tpu_custom_call" | custom-call | tf_op jit(solution)/shard_map/pallas_call | solution.py:683
